TPU v7x, 512 devices: a whole 4x8x8 slice. The times are simulated.
512 devices in a mesh: head: 8 (over z), resp: 64 (over x, y, core).
Axes of the slice: x: 4, y: 8, z: 8, core: 2. Of those that a mesh axis runs over, the one named last changes fastest.
Arguments:
- queries: bfloat16 [8192, 8192], P('resp', 'head'), may hold values from -48 to 48
- response_keys: bfloat16 [8192, 1024], P('resp', 'head'), may hold values from -6 to 6
- response_values: bfloat16 [8192, 1024], P('resp', 'head'), may hold values from -6 to 6
- cotangent: bfloat16 [8192, 8192], P('resp', 'head'), may hold values from -40 to 40
- prefix_keys: bfloat16 [2048, 1024], P(('head', 'resp')), may hold values from -10 to 10
- shared_prefix_values: bfloat16 [2048, 1024], P(('head', 'resp')), may hold values from -6 to 6
- lengths: int32 [64], P('resp'), may hold values from 32 to 128, as said below
- prefix_seen: int32 [64], P('resp'), may hold values from 1024 to 2048, as said below
Outputs:
- grad_queries: bfloat16 [8192, 8192], P('resp', 'head')
- response_key_gradient: bfloat16 [8192, 1024], P('resp', 'head')
- response_value_gradient: bfloat16 [8192, 1024], P('resp', 'head')
- prefix_key_gradient: float32 [2048, 1024], P(('head', 'resp'))
- prefix_value_gradient: float32 [2048, 1024], P(('head', 'resp'))
Inputs may be any that keep to these rules, and one draw needn't show every extreme that they name: `lengths`: one response has all 128 tokens live and one has 32. `prefix_seen`: one response sees the whole prefix and one sees 2048 // 2 positions.
All inputs are finite; a program needn't handle non-finite values.
Results may differ from a plain program's by a relative error of at most 0.011.
Values may be sent and summed in bfloat16 or wider, within the bound.
No kernel may reach another device: no remote copies, remote signals or barrier semaphores. Data moves between devices by JAX's collectives and lax.ppermute only.
A program may use at most 64 MiB of HBM per device.

v0:
```python
import math

import jax
import jax.numpy as jnp
from jax import lax
from jax.sharding import PartitionSpec as P

NEGATIVE = -1e30


def stack_heads(block, group_size):
    rows, columns = block.shape
    head_size = columns // group_size
    return (
        block.reshape(rows, group_size, head_size)
        .transpose(1, 0, 2)
        .reshape(group_size * rows, head_size)
    )


def unstack_heads(block, group_size):
    stacked_rows, head_size = block.shape
    rows = stacked_rows // group_size
    return (
        block.reshape(group_size, rows, head_size)
        .transpose(1, 0, 2)
        .reshape(rows, group_size * head_size)
    )


def per_device(
    queries,
    response_keys,
    response_values,
    cotangent,
    prefix_keys,
    shared_prefix_values,
    lengths,
    prefix_seen,
):
    head_size = response_keys.shape[1]
    token_count = response_keys.shape[0]
    group_size = queries.shape[1] // head_size
    factor = head_size ** (-0.5)
    head_count = lax.axis_size("head")
    resp_count = lax.axis_size("resp")
    local_rows = prefix_keys.shape[0]
    owned_keys, owned_values = (
        lax.all_to_all(prefix_keys, "head", split_axis=1, concat_axis=0, tiled=True),
        lax.all_to_all(shared_prefix_values, "head", split_axis=1, concat_axis=0, tiled=True),
    )
    keys_all, values_all = (
        lax.all_gather(owned_keys, "resp", axis=0, tiled=True),
        lax.all_gather(owned_values, "resp", axis=0, tiled=True),
    )
    prefix_len = keys_all.shape[0]
    block_rows = head_count * local_rows
    prefix_index = jnp.arange(prefix_len, dtype=jnp.int32)
    position = (
        prefix_index // local_rows % head_count * (resp_count * local_rows)
        + prefix_index // block_rows * local_rows
        + prefix_index % local_rows
    )
    visible = position < prefix_seen[0]
    live_rows = jnp.arange(token_count, dtype=jnp.int32) < lengths[0]
    masked_grad = jnp.where(live_rows[:, None], cotangent, jnp.zeros_like(cotangent))
    query_stack = stack_heads(queries, group_size)
    grad_stack = stack_heads(masked_grad, group_size)
    row_token = jnp.arange(group_size * token_count, dtype=jnp.int32) % token_count
    causal = row_token[:, None] >= jnp.arange(token_count, dtype=jnp.int32)[None, :]
    own_scores = jnp.dot(query_stack, response_keys.T, preferred_element_type=jnp.float32) * factor
    own_scores = jnp.where(causal, own_scores, NEGATIVE)
    own_gprobs = jnp.dot(grad_stack, response_values.T, preferred_element_type=jnp.float32)
    block_width = math.gcd(prefix_len, 512)
    block_count = prefix_len // block_width
    blocks = (
        keys_all.reshape(block_count, block_width, head_size),
        values_all.reshape(block_count, block_width, head_size),
        visible.reshape(block_count, block_width),
    )
    row_peak = jnp.max(own_scores, axis=1)
    weights = jnp.exp(own_scores - row_peak[:, None])
    row_total = jnp.sum(weights, axis=1)
    row_weighted = jnp.sum(weights * own_gprobs, axis=1)

    def block_scores(key_block, value_block, seen_block):
        scores = jnp.dot(query_stack, key_block.T, preferred_element_type=jnp.float32) * factor
        scores = jnp.where(seen_block[None, :], scores, NEGATIVE)
        grad_probs = jnp.dot(grad_stack, value_block.T, preferred_element_type=jnp.float32)
        return (scores, grad_probs)

    def stat_step(running, pieces):
        peak_now, total_now, weighted_now = running
        scores, grad_probs = block_scores(pieces[0], pieces[1], pieces[2])
        new_peak = jnp.maximum(peak_now, jnp.max(scores, axis=1))
        rescale = jnp.exp(peak_now - new_peak)
        weights = jnp.exp(scores - new_peak[:, None])
        return (
            (
                new_peak,
                total_now * rescale + jnp.sum(weights, axis=1),
                weighted_now * rescale + jnp.sum(weights * grad_probs, axis=1),
            ),
            None,
        )

    (row_peak, row_total, row_weighted), _ = lax.scan(
        stat_step, (row_peak, row_total, row_weighted), blocks
    )
    log_total = row_peak + jnp.log(row_total)
    delta = row_weighted / row_total

    def block_grads(key_block, value_block, seen_block):
        scores, grad_probs = block_scores(key_block, value_block, seen_block)
        probs = jnp.exp(scores - log_total[:, None])
        grad_scores = probs * (grad_probs - delta[:, None])
        return (probs.astype(jnp.bfloat16), grad_scores.astype(jnp.bfloat16))

    own_probs = jnp.exp(own_scores - log_total[:, None])
    own_gscores = own_probs * (own_gprobs - delta[:, None])
    own_plow = own_probs.astype(jnp.bfloat16)
    own_glow = own_gscores.astype(jnp.bfloat16)
    query_gradient = jnp.dot(own_glow, response_keys, preferred_element_type=jnp.float32)
    grad_own_keys = (
        jnp.dot(own_glow.T, query_stack, preferred_element_type=jnp.float32) * factor
    ).astype(jnp.bfloat16)
    grad_own_values = jnp.dot(own_plow.T, grad_stack, preferred_element_type=jnp.float32).astype(
        jnp.bfloat16
    )

    def grad_step(running, pieces):
        probs_low, grad_low = block_grads(pieces[0], pieces[1], pieces[2])
        key_terms = jnp.dot(grad_low.T, query_stack, preferred_element_type=jnp.float32) * factor
        value_terms = jnp.dot(probs_low.T, grad_stack, preferred_element_type=jnp.float32)
        return (
            running + jnp.dot(grad_low, pieces[0], preferred_element_type=jnp.float32),
            (key_terms, value_terms),
        )

    query_gradient, (key_parts, value_parts) = lax.scan(grad_step, query_gradient, blocks)
    summed_keys, summed_values = (
        lax.psum_scatter(
            key_parts.reshape(prefix_len, head_size), "resp", scatter_dimension=0, tiled=True
        ),
        lax.psum_scatter(
            value_parts.reshape(prefix_len, head_size), "resp", scatter_dimension=0, tiled=True
        ),
    )
    back_keys, back_values = (
        lax.all_to_all(
            summed_keys.astype(jnp.bfloat16), "head", split_axis=0, concat_axis=1, tiled=True
        ).astype(summed_keys.dtype),
        lax.all_to_all(
            summed_values.astype(jnp.bfloat16), "head", split_axis=0, concat_axis=1, tiled=True
        ).astype(summed_values.dtype),
    )
    grad_queries = unstack_heads((query_gradient * factor).astype(jnp.bfloat16), group_size)
    return (grad_queries, grad_own_keys, grad_own_values, back_keys, back_values)


def solution(mesh):
    placed = (
        P("resp", "head"),
        P("resp", "head"),
        P("resp", "head"),
        P("resp", "head"),
        P(("head", "resp"), None),
        P(("head", "resp"), None),
        P("resp"),
        P("resp"),
    )
    return jax.shard_map(
        per_device,
        mesh=mesh,
        in_specs=placed,
        out_specs=(
            P("resp", "head"),
            P("resp", "head"),
            P("resp", "head"),
            P(("head", "resp"), None),
            P(("head", "resp"), None),
        ),
        check_vma=False,
    )
```

profile of v0, /device:TPU:1, one launch (start us, length us, event | category | flops | bytes accessed | tf_op | source)
XLA Modules:
  0.0 467.5 jit_solution(2968470838454422959)
XLA Ops:
  7.2 11.0 %all-to-all-start.1 = ((bf16[4,8,128]{2,0,1:T(4,128)(2,1)}), bf16[4,8,128]{2,0,1:T(4,128)(2,1)S(1)}, u32[]{:S(2)}, u32[]{:S(2)}) async-start(bf16[4,8,128]{2,0,1:T(4,128)(2,1)} %bitcast.137), calls=%async_computation.1 | async-start | bytes 16384 | tf_op jit(solution)/shard_map/all_to_all | solution.py:50
  19.6 1.1 copy_bitcast_fusion.1
  21.7 1.0 multiply_reduce_fusion.1
  22.7 2.0 all-to-all-done.1
  24.8 4.6 all-to-all-start
  29.4 52.6 %all_gather.7 = bf16[2048,128]{1,0:T(8,128)(2,1)S(1)} all-gather(bf16[32,128]{1,0:T(8,128)(2,1)S(1)} %bitcast.135), channel_id=1, replica_groups=mesh['head'=8,'resp'=64] {'resp'}, dimensions={0}, use_global_device_ids=true | all-gather | bytes 532480 | tf_op jit(solution)/shard_map/all_gather | solution.py:54
  82.1 48.8 %all_gather.6 = bf16[2048,128]{1,0:T(8,128)(2,1)S(1)} all-gather(bf16[32,128]{1,0:T(8,128)(2,1)S(1)} %bitcast.136), channel_id=1, replica_groups=mesh['head'=8,'resp'=64] {'resp'}, dimensions={0}, use_global_device_ids=true | all-gather | bytes 532480 | tf_op jit(solution)/shard_map/all_gather | solution.py:53
  130.9 6.8 %while.28 = (s32[]{:T(128)}, f32[1024]{0:T(1024)S(1)}, f32[1024]{0:T(1024)S(1)}, f32[1024]{0:T(1024)S(1)}, pred[4,512]{1,0:T(4,128)(4,1)S(1)}, /*index=5*/bf16[4...) while((s32[]{:T(128)}, f32[1024]{0:T(1024)S(1)}, ...), condition=%wide.region_7.8_spmd, body=%wide.region_3.7_spmd.sunk | while | flops 274729984 | bytes 7154297 | solution.py:107
  138.2 15.8 %while.29 = (s32[]{:T(128)}, f32[1024,128]{1,0:T(8,128)S(1)}, f32[4,512,128]{2,1,0:T(8,128)}, f32[4,512,128]{2,1,0:T(8,128)}, pred[4,512]{1,0:T(4,128)(4,1)S(1)}...) while((s32[]{:T(128)}, f32[1024,128]{1,0:T(8,128)S(1)}, ...), condition=%wide.region_9.10_spmd, body=%wide.region_8.9_spmd.sunk | while | flops 674955264 | bytes 12461717 | solution.py:140
  139.3 1.2 fusion.94
  141.0 1.1 fusion.93
  143.2 1.2 fusion.94
  144.9 1.2 fusion.93
  147.2 1.2 fusion.94
  148.8 1.2 fusion.93
  151.1 1.2 fusion.94
  152.8 1.2 fusion.93
  155.8 138.6 %reduce-scatter.3.cloned.1.call-done = f32[32,128]{1,0:T(8,128)} async-done(((f32[2048,128]{1,0:T(8,128)}), f32[32,128]{1,0:T(8,128)}) %reduce-scatter.3.cloned.1.call-update) | async-done | bytes 16400 | tf_op jit(solution)/shard_map/reduce_scatter | solution.py:142
  294.4 1.3 convert_element_type.50
  295.7 7.0 %all-to-all-start.2 = ((bf16[8,4,128]{2,1,0:T(4,128)(2,1)}), bf16[8,4,128]{2,1,0:T(4,128)(2,1)S(1)}, u32[]{:S(2)}, u32[]{:S(2)}) async-start(bf16[8,4,128]{2,1,0:T(4,128)(2,1)} %bitcast.24), calls=%async_computation.3 | async-start | bytes 16384 | tf_op jit(solution)/shard_map/all_to_all | solution.py:150
  304.6 140.5 %reduce-scatter.5.cloned.1.call-done = f32[32,128]{1,0:T(8,128)} async-done(((f32[2048,128]{1,0:T(8,128)}), f32[32,128]{1,0:T(8,128)}) %reduce-scatter.5.cloned.1.call-update) | async-done | bytes 16400 | tf_op jit(solution)/shard_map/reduce_scatter | solution.py:145
  445.1 1.3 convert_element_type.54
  446.4 7.1 %all-to-all-start.3 = ((bf16[8,4,128]{2,1,0:T(4,128)(2,1)}), bf16[8,4,128]{2,1,0:T(4,128)(2,1)S(1)}, u32[]{:S(2)}, u32[]{:S(2)}) async-start(bf16[8,4,128]{2,1,0:T(4,128)(2,1)} %bitcast.28), calls=%async_computation.5 | async-start | bytes 16384 | tf_op jit(solution)/shard_map/all_to_all | solution.py:153
  454.1 6.0 %all-to-all-done.3 = bf16[8,4,128]{2,1,0:T(4,128)(2,1)S(1)} async-done(((bf16[8,4,128]{2,1,0:T(4,128)(2,1)}), bf16[8,4,128]{2,1,0:T(4,128)(2,1)S(1)}, u32[]{:S(2)}, u32[]{:S(2)}) %all-to-all-start.3) | async-done | bytes 8224 | tf_op jit(solution)/shard_map/all_to_all | solution.py:153
  (73 shorter events, 19.4 us)
Async XLA Ops:
  7.2 12.3 %copy-start = (bf16[128,1024]{1,0:T(8,128)(2,1)S(1)}, bf16[128,1024]{1,0:T(8,128)(2,1)}, u32[]{:S(2)}) copy-start(bf16[128,1024]{1,0:T(8,128)(2,1)} %param.12) | copy-start | bytes 786436
  7.2 17.6 %all-to-all-start.1 = ((bf16[4,8,128]{2,0,1:T(4,128)(2,1)}), bf16[4,8,128]{2,0,1:T(4,128)(2,1)S(1)}, u32[]{:S(2)}, u32[]{:S(2)}) async-start(bf16[4,8,128]{2,0,1:T(4,128)(2,1)} %bitcast.137), calls=%async_computation.1 | async-start | bytes 16384 | tf_op jit(solution)/shard_map/all_to_all | solution.py:50
  24.8 57.3 %all-to-all-start = ((bf16[4,8,128]{2,0,1:T(4,128)(2,1)}), bf16[4,8,128]{2,0,1:T(4,128)(2,1)S(1)}, u32[]{:S(2)}, u32[]{:S(2)}) async-start(bf16[4,8,128]{2,0,1:T(4,128)(2,1)} %bitcast.12), calls=%async_computation | async-start | bytes 16384 | tf_op jit(solution)/shard_map/all_to_all | solution.py:49
  29.4 265.0 %reduce-scatter.3.cloned.1.call-start = ((), (), s32[]{:S(2)}) async-start(), calls=%async_computation.6 | async-start | bytes 1064960 | tf_op jit(solution)/shard_map/reduce_scatter | solution.py:142
  130.9 7.0 %copy-start.1 = (bf16[128,128]{1,0:T(8,128)(2,1)S(1)}, bf16[128,128]{1,0:T(8,128)(2,1)}, u32[]{:S(2)}) copy-start(bf16[128,128]{1,0:T(8,128)(2,1)} %param.13) | copy-start | bytes 98308
  154.0 291.1 %reduce-scatter.5.cloned.1.call-start = ((), (), s32[]{:S(2)}) async-start(), calls=%async_computation.7 | async-start | bytes 1064960 | tf_op jit(solution)/shard_map/reduce_scatter | solution.py:145
  295.7 150.7 %all-to-all-start.2 = ((bf16[8,4,128]{2,1,0:T(4,128)(2,1)}), bf16[8,4,128]{2,1,0:T(4,128)(2,1)S(1)}, u32[]{:S(2)}, u32[]{:S(2)}) async-start(bf16[8,4,128]{2,1,0:T(4,128)(2,1)} %bitcast.24), calls=%async_computation.3 | async-start | bytes 16384 | tf_op jit(solution)/shard_map/all_to_all | solution.py:150
  446.4 13.7 %all-to-all-start.3 = ((bf16[8,4,128]{2,1,0:T(4,128)(2,1)}), bf16[8,4,128]{2,1,0:T(4,128)(2,1)S(1)}, u32[]{:S(2)}, u32[]{:S(2)}) async-start(bf16[8,4,128]{2,1,0:T(4,128)(2,1)} %bitcast.28), calls=%async_computation.5 | async-start | bytes 16384 | tf_op jit(solution)/shard_map/all_to_all | solution.py:153
Sparse Core Ops, SparseCore 0:
  154.1 140.2 reduce-scatter.2
  299.0 146.0 reduce-scatter.4
where the time goes:
time: 474 us; the launch traced here: 468 us
  waiting for transfers between devices  288 us (61%)
  blocking collectives  101 us (21%)
  starting transfers between devices  29.8 us (6%)
  matrix products  23.9 us (5%)
  between operations  15.5 us (3%)
  other arithmetic  7.22 us (2%)
    reduce_scatter x1, waiting for transfers between devices, per_device(): lax.psum_scatter(value_parts.reshape(prefix_len, head_size), 'resp', scat...  140 us
    reduce_scatter x1, waiting for transfers between devices, per_device(): lax.psum_scatter(key_parts.reshape(prefix_len, head_size), 'resp', scatte...  139 us
    all_gather x1, blocking collectives, per_device(): lax.all_gather(owned_values, 'resp', axis=0, tiled=True)  52.6 us
    all_gather x1, blocking collectives, per_device(): lax.all_gather(owned_keys, 'resp', axis=0, tiled=True)  48.8 us
    all_to_all x1, starting transfers between devices, per_device(): lax.all_to_all(shared_prefix_values, 'head', split_axis=1, concat_axis=0,...  11 us
  transfers between devices with their start and end apart: 6, of which 4 were waited for; matrix products, arithmetic and copies ran while one was open for 2% of the time, Pallas kernels for 0%

commit v1 on v0

v1 whole, which is shorter than its diff:
```python
import functools
import math

import jax
import jax.numpy as jnp
from jax import lax
from jax.experimental import pallas as pl
from jax.experimental.pallas import tpu as pltpu
from jax.sharding import Mesh, PartitionSpec as P

NEGATIVE = -1e30
F32 = jnp.float32
BF16 = jnp.bfloat16
TILE = 8
HALF = 4
CORES = 2
VMEM = pl.BlockSpec(memory_space=pltpu.VMEM)
SMEM = pl.BlockSpec(memory_space=pltpu.SMEM)


def dot(a, b, dims):
    return lax.dot_general(a, b, (dims, ((), ())), preferred_element_type=F32)


NT = ((1,), (1,))
NN = ((1,), (0,))


def pack_kernel(keys_ref, values_ref, out_ref, both):
    heads = keys_ref.shape[1] // 128
    span = out_ref.shape[0] // heads
    both[0:HALF, :] = keys_ref[...].astype(F32)
    both[HALF:TILE, :] = values_ref[...].astype(F32)
    for head in range(heads):
        tile = both[:, head * 128 : (head + 1) * 128]
        tiles = jnp.broadcast_to(tile[None], (span // TILE, TILE, 128))
        out_ref[head * span : (head + 1) * span, :] = tiles.reshape(span, 128).astype(BF16)


def split_messages(block):
    count = block.shape[0] // (2 * TILE)
    pairs = block.astype(F32).reshape(count, 2, TILE, 128)
    first, second = pairs[:, 0], pairs[:, 1]
    top = lax.broadcasted_iota(jnp.int32, first.shape, 1) < HALF
    keys = jnp.where(top, first, pltpu.roll(second, HALF, 1))
    values = jnp.where(top, pltpu.roll(first, HALF, 1), second)
    return (
        keys.reshape(count * TILE, 128).astype(BF16),
        values.reshape(count * TILE, 128).astype(BF16),
    )


def join_messages(keys, values):
    count = keys.shape[0] // TILE
    keys = keys.reshape(count, TILE, 128)
    values = values.reshape(count, TILE, 128)
    top = lax.broadcasted_iota(jnp.int32, keys.shape, 1) < HALF
    first = jnp.where(top, keys, pltpu.roll(values, HALF, 1))
    second = jnp.where(top, pltpu.roll(keys, HALF, 1), values)
    pairs = jnp.stack([first, second], axis=1)
    return pairs.reshape(2 * count * TILE, 128).astype(BF16)


def fold(block, op):
    rows, lanes = block.shape
    return op(block.reshape(rows // TILE, TILE, lanes), axis=0)


def grad_kernel(
    length_ref,
    seen_ref,
    q_ref,
    g_ref,
    own_k_ref,
    own_v_ref,
    mine_ref,
    theirs_ref,
    dq_ref,
    dok_ref,
    dov_ref,
    dmine_ref,
    dtheirs_ref,
    k_s,
    v_s,
    kt_s,
    q_s,
    g_s,
    w_s,
    p_s,
    dk_s,
    dv_s,
    *,
    core_axis,
    chunk,
):
    tokens = own_k_ref.shape[0]
    group = q_ref.shape[1] // 128
    half = mine_ref.shape[0] // 2
    key_count = tokens + 2 * half
    factor = 128 ** (-0.5)
    scale = factor * math.log2(math.e)
    length = length_ref[0]
    seen = seen_ref[0]
    core = lax.axis_index(core_axis)

    live = lax.broadcasted_iota(jnp.int32, (tokens, 128), 0) < length
    for head in range(group):
        q_s[head * tokens : (head + 1) * tokens, :] = q_ref[:, head * 128 : (head + 1) * 128]
        grad = g_ref[:, head * 128 : (head + 1) * 128].astype(F32)
        g_s[head * tokens : (head + 1) * tokens, :] = jnp.where(live, grad, 0.0).astype(BF16)
    k_s[0:tokens, :] = own_k_ref[...]
    v_s[0:tokens, :] = own_v_ref[...]
    kt_s[:, 0:tokens] = own_k_ref[...].astype(F32).T.astype(BF16)
    step = 256
    for block, ref in enumerate((mine_ref, theirs_ref)):
        for at in range(0, half, step):
            keys, values = split_messages(ref[2 * at : 2 * (at + step), :])
            row = tokens + block * half + at
            k_s[row : row + step, :] = keys
            v_s[row : row + step, :] = values
            kt_s[:, row : row + step] = keys.astype(F32).T.astype(BF16)

    lanes = 2 * tokens
    starts = [(0, tokens)] + [(row, chunk) for row in range(tokens, key_count, chunk)]

    def pair_body(pair, first):
        rows = pl.ds(pl.multiple_of(pair * lanes, lanes), lanes)
        q2 = q_s[rows, :]
        g2 = g_s[rows, :]
        peak = jnp.full((TILE, lanes), NEGATIVE, F32)
        for row, size in starts:
            s = dot(k_s[row : row + size, :], q2, NT)
            index = lax.broadcasted_iota(jnp.int32, (size, lanes), 0)
            if row == 0:
                token = lax.broadcasted_iota(jnp.int32, (size, lanes), 1) % tokens
                keep = index <= token
            else:
                block = (row - tokens) // half
                local = index + (row - tokens - block * half)
                side = core if block == 0 else 1 - core
                keep = (local // HALF) * TILE + local % HALF + side * HALF < seen
            s = jnp.where(keep, s, NEGATIVE)
            w_s[row : row + size, :] = s
            peak = jnp.maximum(peak, fold(s, jnp.max))
        peak = jnp.max(peak, axis=0, keepdims=True)
        total = jnp.zeros((TILE, lanes), F32)
        weighted = jnp.zeros((TILE, lanes), F32)
        for row, size in starts:
            gp = dot(v_s[row : row + size, :], g2, NT)
            w = jnp.exp2((w_s[row : row + size, :] - peak) * scale)
            w_s[row : row + size, :] = w
            p_s[row : row + size, :] = gp
            total = total + fold(w, jnp.sum)
            weighted = weighted + fold(w * gp, jnp.sum)
        inverse = 1.0 / jnp.sum(total, axis=0, keepdims=True)
        delta = jnp.sum(weighted, axis=0, keepdims=True) * inverse
        dqt = jnp.zeros((128, lanes), F32)
        for row, size in starts:
            probs = w_s[row : row + size, :] * inverse
            grads = probs * (p_s[row : row + size, :] - delta)
            probs = probs.astype(BF16)
            grads = grads.astype(BF16)
            dqt = dqt + dot(kt_s[:, row : row + size], grads, NN)
            dk = dot(grads, q2, NN)
            dv = dot(probs, g2, NN)
            if first:
                dk_s[row : row + size, :] = dk
                dv_s[row : row + size, :] = dv
            else:
                dk_s[row : row + size, :] += dk
                dv_s[row : row + size, :] += dv
        dqt = dqt * factor
        for sub in range(2):
            block = dqt[:, sub * tokens : (sub + 1) * tokens].T.astype(BF16)
            dq_ref[:, pl.ds(pl.multiple_of((pair * 2 + sub) * 128, 128), 128)] = block

    pair_body(0, True)

    def loop_body(pair, carry):
        pair_body(pair, False)
        return carry

    lax.fori_loop(1, group // 2, loop_body, 0)

    dok_ref[...] = (dk_s[0:tokens, :] * factor).astype(BF16)
    dov_ref[...] = dv_s[0:tokens, :].astype(BF16)
    for block, ref in enumerate((dmine_ref, dtheirs_ref)):
        for at in range(0, half, step):
            row = tokens + block * half + at
            ref[2 * at : 2 * (at + step), :] = join_messages(
                dk_s[row : row + step, :] * factor, dv_s[row : row + step, :]
            )


def sum_kernel(in_ref, keys_ref, values_ref):
    heads = keys_ref.shape[1] // 128
    span = in_ref.shape[0] // heads
    for head in range(heads):
        part = in_ref[head * span : (head + 1) * span, :].astype(F32)
        total = jnp.sum(part.reshape(span // TILE, TILE, 128), axis=0)
        keys_ref[:, head * 128 : (head + 1) * 128] = total[0:HALF, :]
        values_ref[:, head * 128 : (head + 1) * 128] = total[HALF:TILE, :]


def swap_cores(block):
    return lax.ppermute(block, "core", [(0, 1), (1, 0)])


def per_device(queries, own_keys, own_values, cotangent, prefix_keys, prefix_values, lengths, seen):
    tokens = own_keys.shape[0]
    group = queries.shape[1] // 128
    wide = ("head", "x", "y")
    peers = math.prod(lax.axis_size(axis) for axis in wide)
    rows = peers * TILE
    half = peers * HALF
    key_count = tokens + 2 * half
    messages = pl.pallas_call(
        pack_kernel,
        out_shape=jax.ShapeDtypeStruct((rows, 128), BF16),
        in_specs=[VMEM] * 2,
        out_specs=VMEM,
        scratch_shapes=[pltpu.VMEM((TILE, prefix_keys.shape[1]), F32)],
    )(prefix_keys, prefix_values)
    mine = lax.all_to_all(messages, wide, 0, 0, tiled=True)
    theirs = swap_cores(mine)
    dq, dok, dov, dmine, dtheirs = pl.pallas_call(
        functools.partial(grad_kernel, core_axis="core", chunk=256),
        out_shape=(
            jax.ShapeDtypeStruct(queries.shape, BF16),
            jax.ShapeDtypeStruct(own_keys.shape, BF16),
            jax.ShapeDtypeStruct(own_values.shape, BF16),
            jax.ShapeDtypeStruct((rows, 128), BF16),
            jax.ShapeDtypeStruct((rows, 128), BF16),
        ),
        in_specs=[SMEM] * 2 + [VMEM] * 6,
        out_specs=(VMEM,) * 5,
        scratch_shapes=[
            pltpu.VMEM((key_count, 128), BF16),
            pltpu.VMEM((key_count, 128), BF16),
            pltpu.VMEM((128, key_count), BF16),
            pltpu.VMEM((group * tokens, 128), BF16),
            pltpu.VMEM((group * tokens, 128), BF16),
            pltpu.VMEM((key_count, 2 * tokens), F32),
            pltpu.VMEM((key_count, 2 * tokens), F32),
            pltpu.VMEM((key_count, 128), F32),
            pltpu.VMEM((key_count, 128), F32),
        ],
        compiler_params=pltpu.CompilerParams(vmem_limit_bytes=40 * 1024 * 1024),
    )(lengths, seen, queries, cotangent, own_keys, own_values, mine, theirs)
    summed = (dmine.astype(F32) + swap_cores(dtheirs).astype(F32)).astype(BF16)
    back = lax.all_to_all(summed, wide, 0, 0, tiled=True)
    dkeys, dvalues = pl.pallas_call(
        sum_kernel,
        out_shape=(jax.ShapeDtypeStruct(prefix_keys.shape, F32),) * 2,
        in_specs=[VMEM],
        out_specs=(VMEM,) * 2,
    )(back)
    return dq, dok, dov, dkeys, dvalues


def solution(mesh):
    heads, responses = mesh.devices.shape
    y_size = 8
    x_size = responses // (y_size * CORES)
    split = Mesh(
        mesh.devices.reshape(heads, x_size, y_size, CORES), ("head", "x", "y", "core")
    )
    resp = ("x", "y", "core")
    spread = ("head", "x", "y", "core")
    return jax.shard_map(
        per_device,
        mesh=split,
        in_specs=(
            P(resp, "head"),
            P(resp, "head"),
            P(resp, "head"),
            P(resp, "head"),
            P(spread, None),
            P(spread, None),
            P(resp),
            P(resp),
        ),
        out_specs=(
            P(resp, "head"),
            P(resp, "head"),
            P(resp, "head"),
            P(spread, None),
            P(spread, None),
        ),
        check_vma=False,
    )
```

time: 474 us -> 96.1 us (0.20); the launches traced: 468 us -> 95.7 us
  waiting for transfers between devices: 288 us -> 1.74 us
  blocking collectives: 101 us -> 72.4 us
  matrix products: 23.9 us -> 0 us
  starting transfers between devices: 29.8 us -> 6.83 us
  between operations: 15.5 us -> 1.96 us
  Pallas kernels: 0 us -> 12.7 us
  other arithmetic: 7.22 us -> 0.14 us
    reduce_scatter x2 -> x0, waiting for transfers between devices: 279 us -> none  [the longest x1 140 us: per_device(): lax.psum_scatter(value_parts.reshape(prefix_len, head_size), 'resp', scat...]
    all_gather x2 -> x0, blocking collectives: 101 us -> none  [the longest x1 52.6 us: per_device(): lax.all_gather(owned_values, 'resp', axis=0, tiled=True)]
    all_to_all x0 -> x2, blocking collectives: none -> 72.4 us  [the longest x1 42.7 us: per_device(): mine = lax.all_to_all(messages, wide, 0, 0, tiled=True)]
    all_to_all x4 -> x0, starting transfers between devices: 29.7 us -> none  [the longest x1 11 us: per_device(): lax.all_to_all(shared_prefix_values, 'head', split_axis=1, concat_axis=0,...]
    dot_general x33 -> x0, matrix products: 23.9 us -> none  [the longest x4 4.69 us: grad_step(): jnp.dot(probs_low.T, grad_stack, preferred_element_type=jnp.float32)]
    pallas_call x0 -> x3, Pallas kernels: none -> 12.7 us  [the longest x1 9.39 us: per_device(): pl.pallas_call(functools.partial(grad_kernel, core_axis='core', chunk=256...]
    all_to_all x4 -> x0, waiting for transfers between devices: 8 us -> none  [the longest x1 5.97 us: per_device(): lax.all_to_all(summed_values.astype(jnp.bfloat16), 'head', split_axis=0,...]
    ppermute x0 -> x2, starting transfers between devices: none -> 6.83 us  [swap_cores(): return lax.ppermute(block, 'core', [(0, 1), (1, 0)])]
  transfers between devices with their start and end apart: 6 -> 2, of which waited for: 4 -> 2; matrix products, arithmetic and copies ran while one was open for 2% -> 0% of each run, Pallas kernels for 0% -> 0%
where the time goes in v1:
time: 96.1 us; the launch traced here: 95.7 us
  blocking collectives  72.4 us (75%)
  Pallas kernels  12.7 us (13%)
  starting transfers between devices  6.83 us (7%)
  between operations  1.96 us (2%)
  waiting for transfers between devices  1.74 us (2%)
    all_to_all x1, blocking collectives, per_device(): mine = lax.all_to_all(messages, wide, 0, 0, tiled=True)  42.7 us
    all_to_all x1, blocking collectives, per_device(): back = lax.all_to_all(summed, wide, 0, 0, tiled=True)  29.7 us
    pallas_call x1, Pallas kernels, per_device(): pl.pallas_call(functools.partial(grad_kernel, core_axis='core', chunk=256...  9.39 us
    ppermute x2, starting transfers between devices, swap_cores(): return lax.ppermute(block, 'core', [(0, 1), (1, 0)])  6.83 us
  transfers between devices with their start and end apart: 2, of which 2 were waited for; matrix products, arithmetic and copies ran while one was open for 0% of the time, Pallas kernels for 0%

profile of v1, /device:TPU:1, one launch (start us, length us, event | category | flops | bytes accessed | tf_op | source)
XLA Modules:
  0.0 95.7 jit_solution(17339169901289681253)
XLA Ops:
  0.6 1.5 %shard_map.119 = bf16[2048,128]{1,0:T(8,128)(2,1)} custom-call(bf16[4,1024]{1,0:T(4,128)(2,1)} %keys_ref.1, bf16[4,1024]{1,0:T(4,128)(2,1)} %values_ref.1), custom_call_target="tpu_custom_call" | custom-call | tf_op jit(solution)/shard_map/pallas_call | solution.py:217
  2.2 0.0 copy-start
  2.2 0.0 copy-start.1
  2.2 0.0 copy-start.2
  2.2 0.0 copy-start.3
  2.2 42.7 %all_to_all.22 = bf16[256,8,128]{2,1,0:T(8,128)(2,1)S(1)} all-to-all(bf16[256,8,128]{2,1,0:T(8,128)(2,1)} %bitcast.8), channel_id=1, replica_groups=mesh['head'=8,'x'=4,'y'=8,'core'=2] {'head','x','y'}, dimensions={0} | all-to-all | bytes 1048576 | tf_op jit(solution)/shard_map/all_to_all | solution.py:224
  44.9 4.6 %collective-permute-start = (bf16[2048,128]{1,0:T(8,128)(2,1)S(1)}, bf16[2048,128]{1,0:T(8,128)(2,1)S(1)}, u32[]{:S(2)}, u32[]{:S(2)}) collective-permute-start(bf16[2048,128]{1,0:T(8,128)(2,1)S(1)} %bitcast.5), channel_id=1, source_target_pairs={{0,1},{1,0},{2,3},{3,2},{4,5},{5,4},{6,7},{7,6},{8,9},{9,8},{10,11... | collective-permute-start | bytes 1572872 | tf_op jit(solution)/shard_map/ppermute | solution.py:206
  50.8 0.2 collective-permute-done.theirs_ref
  51.0 0.0 copy-done
  51.0 0.0 copy-done.1
  51.0 0.0 copy-done.2
  51.0 0.0 copy-done.3
  51.0 9.4 %shard_map.120 = (bf16[128,1024]{1,0:T(8,128)(2,1)}, bf16[128,128]{1,0:T(8,128)(2,1)}, bf16[128,128]{1,0:T(8,128)(2,1)}, bf16[2048,128]{1,0:T(8,128)(2,1)S(1)}, bf16[2048,128]{1,0:T(8,128)(2,1)S(1)}) custom-call(s32[1]{0:T(128)S(6)} %copy.13.length_ref, s32[1]{0:T(128)S(6)} %copy.14.seen_ref, bf16[128,1024]{1,0:T(8,128)(2,1)S(1)} %copy-done, ...), custom_call_target="tpu_custom_call" | custom-call | tf_op jit(solution)/shard_map/pallas_call | solution.py:226
  60.4 2.3 %collective-permute-start.1 = (bf16[2048,128]{1,0:T(8,128)(2,1)S(1)}, bf16[2048,128]{1,0:T(8,128)(2,1)S(1)}, u32[]{:S(2)}, u32[]{:S(2)}) collective-permute-start(bf16[2048,128]{1,0:T(8,128)(2,1)S(1)} %get-tuple-element.16), channel_id=1, source_target_pairs={{0,1},{1,0},{2,3},{3,2},{4,5},{5,4},{6,7},{7,6},{8,9},{9,8},{10,11... | collective-permute-start | bytes 1572872 | tf_op jit(solution)/shard_map/ppermute | solution.py:206
  62.7 1.5 %collective-permute-done.1 = bf16[2048,128]{1,0:T(8,128)(2,1)S(1)} collective-permute-done((bf16[2048,128]{1,0:T(8,128)(2,1)S(1)}, bf16[2048,128]{1,0:T(8,128)(2,1)S(1)}, u32[]{:S(2)}, u32[]{:S(2)}) %collective-permute-start.1) | collective-permute-done | bytes 524320 | tf_op jit(solution)/shard_map/ppermute | solution.py:206
  64.2 0.1 fusion
  64.3 29.7 %all_to_all.23 = bf16[256,8,128]{2,1,0:T(8,128)(2,1)} all-to-all(bf16[256,8,128]{2,1,0:T(8,128)(2,1)S(1)} %fusion), channel_id=1, replica_groups=mesh['head'=8,'x'=4,'y'=8,'core'=2] {'head','x','y'}, dimensions={0} | all-to-all | bytes 1048576 | tf_op jit(solution)/shard_map/all_to_all | solution.py:251
  94.0 1.7 %shard_map.121 = (f32[4,1024]{1,0:T(4,128)}, f32[4,1024]{1,0:T(4,128)}) custom-call(bf16[2048,128]{1,0:T(8,128)(2,1)} %bitcast.7), custom_call_target="tpu_custom_call" | custom-call | tf_op jit(solution)/shard_map/pallas_call | solution.py:252
Async XLA Ops:
  2.2 48.8 %copy-start = (bf16[128,1024]{1,0:T(8,128)(2,1)S(1)}, bf16[128,1024]{1,0:T(8,128)(2,1)}, u32[]{:S(2)}) copy-start(bf16[128,1024]{1,0:T(8,128)(2,1)} %q_ref.1) | copy-start | bytes 786436
  2.2 48.8 %copy-start.1 = (bf16[128,1024]{1,0:T(8,128)(2,1)S(1)}, bf16[128,1024]{1,0:T(8,128)(2,1)}, u32[]{:S(2)}) copy-start(bf16[128,1024]{1,0:T(8,128)(2,1)} %g_ref.1) | copy-start | bytes 786436
  2.2 48.8 %copy-start.2 = (bf16[128,128]{1,0:T(8,128)(2,1)S(1)}, bf16[128,128]{1,0:T(8,128)(2,1)}, u32[]{:S(2)}) copy-start(bf16[128,128]{1,0:T(8,128)(2,1)} %own_k_ref.1) | copy-start | bytes 98308
  2.2 48.8 %copy-start.3 = (bf16[128,128]{1,0:T(8,128)(2,1)S(1)}, bf16[128,128]{1,0:T(8,128)(2,1)}, u32[]{:S(2)}) copy-start(bf16[128,128]{1,0:T(8,128)(2,1)} %own_v_ref.1) | copy-start | bytes 98308
  44.9 6.1 %collective-permute-start = (bf16[2048,128]{1,0:T(8,128)(2,1)S(1)}, bf16[2048,128]{1,0:T(8,128)(2,1)S(1)}, u32[]{:S(2)}, u32[]{:S(2)}) collective-permute-start(bf16[2048,128]{1,0:T(8,128)(2,1)S(1)} %bitcast.5), channel_id=1, source_target_pairs={{0,1},{1,0},{2,3},{3,2},{4,5},{5,4},{6,7},{7,6},{8,9},{9,8},{10,11... | collective-permute-start | bytes 1572872 | tf_op jit(solution)/shard_map/ppermute | solution.py:206
  60.4 3.8 %collective-permute-start.1 = (bf16[2048,128]{1,0:T(8,128)(2,1)S(1)}, bf16[2048,128]{1,0:T(8,128)(2,1)S(1)}, u32[]{:S(2)}, u32[]{:S(2)}) collective-permute-start(bf16[2048,128]{1,0:T(8,128)(2,1)S(1)} %get-tuple-element.16), channel_id=1, source_target_pairs={{0,1},{1,0},{2,3},{3,2},{4,5},{5,4},{6,7},{7,6},{8,9},{9,8},{10,11... | collective-permute-start | bytes 1572872 | tf_op jit(solution)/shard_map/ppermute | solution.py:206

commit v2 on v1

v2 whole, which is shorter than its diff:
```python
import functools
import math

import jax
import jax.numpy as jnp
from jax import lax
from jax.experimental import pallas as pl
from jax.experimental.pallas import tpu as pltpu
from jax.sharding import Mesh, PartitionSpec as P

NEGATIVE = -1e30
F32 = jnp.float32
BF16 = jnp.bfloat16
TILE = 8
HALF = 4
CORES = 2
VMEM = pl.BlockSpec(memory_space=pltpu.VMEM)


def dot(a, b, dims):
    return lax.dot_general(a, b, (dims, ((), ())), preferred_element_type=F32)


NT = ((1,), (1,))
NN = ((1,), (0,))


def pack_kernel(keys_ref, values_ref, out_ref, both):
    heads = keys_ref.shape[1] // 128
    span = out_ref.shape[0] // heads
    both[0:HALF, :] = keys_ref[...].astype(F32)
    both[HALF:TILE, :] = values_ref[...].astype(F32)
    for head in range(heads):
        tile = both[:, head * 128 : (head + 1) * 128]
        tiles = jnp.broadcast_to(tile[None], (span // TILE, TILE, 128))
        out_ref[head * span : (head + 1) * span, :] = tiles.reshape(span, 128).astype(BF16)


def split_messages(block):
    count = block.shape[0] // (2 * TILE)
    pairs = block.astype(F32).reshape(count, 2, TILE, 128)
    first, second = pairs[:, 0], pairs[:, 1]
    top = lax.broadcasted_iota(jnp.int32, first.shape, 1) < HALF
    keys = jnp.where(top, first, pltpu.roll(second, HALF, 1))
    values = jnp.where(top, pltpu.roll(first, HALF, 1), second)
    return (
        keys.reshape(count * TILE, 128).astype(BF16),
        values.reshape(count * TILE, 128).astype(BF16),
    )


def join_messages(keys, values):
    count = keys.shape[0] // TILE
    keys = keys.reshape(count, TILE, 128)
    values = values.reshape(count, TILE, 128)
    top = lax.broadcasted_iota(jnp.int32, keys.shape, 1) < HALF
    first = jnp.where(top, keys, pltpu.roll(values, HALF, 1))
    second = jnp.where(top, pltpu.roll(keys, HALF, 1), values)
    pairs = jnp.stack([first, second], axis=1)
    return pairs.reshape(2 * count * TILE, 128).astype(BF16)


def fold(block, op):
    rows, lanes = block.shape
    return op(block.reshape(rows // TILE, TILE, lanes), axis=0)


def stack_kernel(length_ref, q_ref, g_ref, q_out, g_out):
    tokens = q_ref.shape[0]
    live = lax.broadcasted_iota(jnp.int32, (tokens, 128), 0) < length_ref[...]
    for head in range(q_ref.shape[1] // 128):
        rows = slice(head * tokens, (head + 1) * tokens)
        q_out[rows, :] = q_ref[:, head * 128 : (head + 1) * 128]
        grad = g_ref[:, head * 128 : (head + 1) * 128].astype(F32)
        g_out[rows, :] = jnp.where(live, grad, 0.0).astype(BF16)


def grad_kernel(
    seen_ref,
    q_ref,
    g_ref,
    own_k_ref,
    own_v_ref,
    mine_ref,
    theirs_ref,
    dq_ref,
    dok_ref,
    dov_ref,
    dmine_ref,
    dtheirs_ref,
    k_s,
    v_s,
    kt_s,
    w_s,
    p_s,
    dk_s,
    dv_s,
    *,
    core_axis,
    chunk,
    span,
):
    tokens = own_k_ref.shape[0]
    group = q_ref.shape[0] // tokens
    half = mine_ref.shape[0] // 2
    key_count = tokens + 2 * half
    factor = 128 ** (-0.5)
    scale = factor * math.log2(math.e)
    core = lax.axis_index(core_axis)

    k_s[0:tokens, :] = own_k_ref[...]
    v_s[0:tokens, :] = own_v_ref[...]
    kt_s[:, 0:tokens] = own_k_ref[...].astype(F32).T.astype(BF16)
    step = 256
    for block, ref in enumerate((mine_ref, theirs_ref)):
        for at in range(0, half, step):
            keys, values = split_messages(ref[2 * at : 2 * (at + step), :])
            row = tokens + block * half + at
            k_s[row : row + step, :] = keys
            v_s[row : row + step, :] = values
            kt_s[:, row : row + step] = keys.astype(F32).T.astype(BF16)

    lanes = span * tokens
    starts = [(0, tokens)] + [(row, chunk) for row in range(tokens, key_count, chunk)]
    inner = lax.broadcasted_iota(jnp.int32, (TILE, lanes), 0)
    spread = (inner // HALF) * TILE + inner % HALF
    seen = jnp.broadcast_to(seen_ref[...], (TILE, lanes))
    room = (seen - spread - core * HALF, seen - spread - (1 - core) * HALF)

    def hide(s, row, size):
        if row == 0:
            token = lax.broadcasted_iota(jnp.int32, (size, lanes), 1) % tokens
            index = lax.broadcasted_iota(jnp.int32, (size, lanes), 0)
            return jnp.where(index <= token, s, NEGATIVE)
        block = (row - tokens) // half
        local = row - tokens - block * half
        if local + size <= half // 2:
            return s
        count = size // TILE
        parts = s.reshape(count, TILE, lanes)
        place = 2 * (local + TILE * lax.broadcasted_iota(jnp.int32, parts.shape, 0))
        return jnp.where(place < room[block][None], parts, NEGATIVE).reshape(size, lanes)

    pairs = group // span

    class Block:
        def __init__(self, pair):
            self.pair = pair
            rows = slice(pair * lanes, (pair + 1) * lanes)
            self.rows = rows
            self.w, self.p = w_s.at[pair % 2], p_s.at[pair % 2]
            self.q, self.g = q_ref[rows, :], g_ref[rows, :]
            self.peak = jnp.full((TILE, lanes), NEGATIVE, F32)
            self.total = jnp.zeros((TILE, lanes), F32)
            self.weighted = jnp.zeros((TILE, lanes), F32)
            self.dqt = jnp.zeros((128, lanes), F32)

        def score(self, row, size):
            s = hide(dot(k_s[row : row + size, :], self.q, NT), row, size)
            self.w[row : row + size, :] = s
            self.peak = jnp.maximum(self.peak, fold(s, jnp.max))

        def top(self):
            self.peak = jnp.max(self.peak, axis=0, keepdims=True)

        def weigh(self, row, size):
            gp = dot(v_s[row : row + size, :], self.g, NT)
            w = jnp.exp2((self.w[row : row + size, :] - self.peak) * scale)
            self.w[row : row + size, :] = w
            self.p[row : row + size, :] = gp
            self.total = self.total + fold(w, jnp.sum)
            self.weighted = self.weighted + fold(w * gp, jnp.sum)

        def norm(self):
            self.inverse = 1.0 / jnp.sum(self.total, axis=0, keepdims=True)
            self.delta = jnp.sum(self.weighted, axis=0, keepdims=True) * self.inverse

        def grad(self, row, size):
            probs = self.w[row : row + size, :] * self.inverse
            grads = probs * (self.p[row : row + size, :] - self.delta)
            probs = probs.astype(BF16)
            grads = grads.astype(BF16)
            self.dqt = self.dqt + dot(kt_s[:, row : row + size], grads, NN)
            dk = dot(grads, self.q, NN)
            dv = dot(probs, self.g, NN)
            if self.pair == 0:
                dk_s[row : row + size, :] = dk
                dv_s[row : row + size, :] = dv
            else:
                dk_s[row : row + size, :] += dk
                dv_s[row : row + size, :] += dv

        def finish(self):
            dqt = self.dqt * factor
            for sub in range(span):
                head = self.pair * span + sub
                block = dqt[:, sub * tokens : (sub + 1) * tokens].T.astype(BF16)
                dq_ref[:, head * 128 : (head + 1) * 128] = block

    done = None
    for pair in range(pairs + 1):
        work = Block(pair) if pair < pairs else None
        if work:
            for at in starts:
                work.score(*at)
            work.top()
        for at in starts:
            if work:
                work.weigh(*at)
            if done:
                done.grad(*at)
        if work:
            work.norm()
        if done:
            done.finish()
        done = work

    dok_ref[...] = (dk_s[0:tokens, :] * factor).astype(BF16)
    dov_ref[...] = dv_s[0:tokens, :].astype(BF16)
    for block, ref in enumerate((dmine_ref, dtheirs_ref)):
        for at in range(0, half, step):
            row = tokens + block * half + at
            ref[2 * at : 2 * (at + step), :] = join_messages(
                dk_s[row : row + step, :] * factor, dv_s[row : row + step, :]
            )


def megabytes(count):
    return pltpu.CompilerParams(vmem_limit_bytes=count * 1024 * 1024)


def stack_call(lengths, queries, cotangent):
    tokens, width = queries.shape
    return pl.pallas_call(
        stack_kernel,
        out_shape=(jax.ShapeDtypeStruct((tokens * (width // 128), 128), BF16),) * 2,
        in_specs=[VMEM] * 3,
        out_specs=(VMEM,) * 2,
        compiler_params=megabytes(4),
    )(lengths.reshape(1, 1), queries, cotangent)


def grad_call(seen, q, g, own_keys, own_values, mine, theirs, chunk=512, span=4):
    tokens = own_keys.shape[0]
    stacked = q.shape[0]
    key_count = tokens + mine.shape[0]
    return pl.pallas_call(
        functools.partial(grad_kernel, core_axis="core", chunk=chunk, span=span),
        out_shape=(
            jax.ShapeDtypeStruct((tokens, stacked // tokens * 128), BF16),
            jax.ShapeDtypeStruct(own_keys.shape, BF16),
            jax.ShapeDtypeStruct(own_values.shape, BF16),
            jax.ShapeDtypeStruct(mine.shape, BF16),
            jax.ShapeDtypeStruct(theirs.shape, BF16),
        ),
        in_specs=[VMEM] * 7,
        out_specs=(VMEM,) * 5,
        scratch_shapes=[
            pltpu.VMEM((key_count, 128), BF16),
            pltpu.VMEM((key_count, 128), BF16),
            pltpu.VMEM((128, key_count), BF16),
            pltpu.VMEM((2, key_count, span * tokens), F32),
            pltpu.VMEM((2, key_count, span * tokens), F32),
            pltpu.VMEM((key_count, 128), F32),
            pltpu.VMEM((key_count, 128), F32),
        ],
        compiler_params=megabytes(40),
    )(seen.reshape(1, 1), q, g, own_keys, own_values, mine, theirs)


def sum_kernel(in_ref, keys_ref, values_ref):
    heads = keys_ref.shape[1] // 128
    span = in_ref.shape[0] // heads
    for head in range(heads):
        part = in_ref[head * span : (head + 1) * span, :].astype(F32)
        total = jnp.sum(part.reshape(span // TILE, TILE, 128), axis=0)
        keys_ref[:, head * 128 : (head + 1) * 128] = total[0:HALF, :]
        values_ref[:, head * 128 : (head + 1) * 128] = total[HALF:TILE, :]


def swap_cores(block):
    return lax.ppermute(block, "core", [(0, 1), (1, 0)])


def per_device(queries, own_keys, own_values, cotangent, prefix_keys, prefix_values, lengths, seen):
    wide = ("head", "x", "y")
    peers = math.prod(lax.axis_size(axis) for axis in wide)
    rows = peers * TILE
    messages = pl.pallas_call(
        pack_kernel,
        out_shape=jax.ShapeDtypeStruct((rows, 128), BF16),
        in_specs=[VMEM] * 2,
        out_specs=VMEM,
        scratch_shapes=[pltpu.VMEM((TILE, prefix_keys.shape[1]), F32)],
    )(prefix_keys, prefix_values)
    mine = lax.all_to_all(messages, wide, 0, 0, tiled=True)
    q, g = stack_call(lengths, queries, cotangent)
    theirs = swap_cores(mine)
    dq, dok, dov, dmine, dtheirs = grad_call(
        seen, q, g, own_keys, own_values, mine, theirs
    )
    summed = (dmine.astype(F32) + swap_cores(dtheirs).astype(F32)).astype(BF16)
    back = lax.all_to_all(summed, wide, 0, 0, tiled=True)
    dkeys, dvalues = pl.pallas_call(
        sum_kernel,
        out_shape=(jax.ShapeDtypeStruct(prefix_keys.shape, F32),) * 2,
        in_specs=[VMEM],
        out_specs=(VMEM,) * 2,
        compiler_params=megabytes(4),
    )(back)
    return dq, dok, dov, dkeys, dvalues


def solution(mesh):
    heads, responses = mesh.devices.shape
    y_size = 8
    x_size = responses // (y_size * CORES)
    split = Mesh(
        mesh.devices.reshape(heads, x_size, y_size, CORES), ("head", "x", "y", "core")
    )
    resp = ("x", "y", "core")
    spread = ("head", "x", "y", "core")
    return jax.shard_map(
        per_device,
        mesh=split,
        in_specs=(
            P(resp, "head"),
            P(resp, "head"),
            P(resp, "head"),
            P(resp, "head"),
            P(spread, None),
            P(spread, None),
            P(resp),
            P(resp),
        ),
        out_specs=(
            P(resp, "head"),
            P(resp, "head"),
            P(resp, "head"),
            P(spread, None),
            P(spread, None),
        ),
        check_vma=False,
    )
```

time: 96.1 us -> 94.3 us (0.981)
  Pallas kernels: 12.7 us -> 10.7 us
    pallas_call x1, Pallas kernels: 1.74 us -> 0.7 us  [per_device(): pl.pallas_call(sum_kernel, out_shape=(jax.ShapeDtypeStruct(prefix_keys.sh...]
    pallas_call x1 -> x2, Pallas kernels: 9.39 us -> 8.43 us  [the longest x1 8.3 us: grad_call(): pl.pallas_call(functools.partial(grad_kernel, core_axis='core', chunk=chu...]
where the time goes in v2:
time: 94.3 us; the launch traced here: 93.8 us
  blocking collectives  72 us (76%)
  Pallas kernels  10.7 us (11%)
  starting transfers between devices  6.46 us (7%)
  between operations  1.99 us (2%)
  waiting for transfers between devices  1.93 us (2%)
    all_to_all x1, blocking collectives, per_device(): mine = lax.all_to_all(messages, wide, 0, 0, tiled=True)  42.7 us
    all_to_all x1, blocking collectives, per_device(): back = lax.all_to_all(summed, wide, 0, 0, tiled=True)  29.4 us
    pallas_call x1, Pallas kernels, grad_call(): pl.pallas_call(functools.partial(grad_kernel, core_axis='core', chunk=chu...  8.3 us
    ppermute x2, starting transfers between devices, swap_cores(): return lax.ppermute(block, 'core', [(0, 1), (1, 0)])  6.46 us
    ppermute x2, waiting for transfers between devices, swap_cores(): return lax.ppermute(block, 'core', [(0, 1), (1, 0)])  1.93 us
  transfers between devices with their start and end apart: 2, of which 2 were waited for; matrix products, arithmetic and copies ran while one was open for 0% of the time, Pallas kernels for 0%

profile of v2, /device:TPU:1, one launch (start us, length us, event | category | flops | bytes accessed | tf_op | source)
XLA Modules:
  0.0 93.8 jit_solution(8190291844277506971)
XLA Ops:
  0.6 1.6 %shard_map.120 = bf16[2048,128]{1,0:T(8,128)(2,1)} custom-call(bf16[4,1024]{1,0:T(4,128)(2,1)} %keys_ref.1, bf16[4,1024]{1,0:T(4,128)(2,1)} %values_ref.1), custom_call_target="tpu_custom_call" | custom-call | tf_op jit(solution)/shard_map/pallas_call | solution.py:289
  2.2 0.0 copy-start
  2.2 0.0 copy-start.1
  2.2 42.7 %all_to_all.22 = bf16[256,8,128]{2,1,0:T(8,128)(2,1)S(1)} all-to-all(bf16[256,8,128]{2,1,0:T(8,128)(2,1)} %bitcast.12), channel_id=1, replica_groups=mesh['head'=8,'x'=4,'y'=8,'core'=2] {'head','x','y'}, dimensions={0} | all-to-all | bytes 1048576 | tf_op jit(solution)/shard_map/all_to_all | solution.py:296
  44.9 4.6 %collective-permute-start = (bf16[2048,128]{1,0:T(8,128)(2,1)S(1)}, bf16[2048,128]{1,0:T(8,128)(2,1)S(1)}, u32[]{:S(2)}, u32[]{:S(2)}) collective-permute-start(bf16[2048,128]{1,0:T(8,128)(2,1)S(1)} %bitcast.9), channel_id=1, source_target_pairs={{0,1},{1,0},{2,3},{3,2},{4,5},{5,4},{6,7},{7,6},{8,9},{9,8},{10,11... | collective-permute-start | bytes 1572872 | tf_op jit(solution)/shard_map/ppermute | solution.py:282
  50.8 0.0 copy-done
  50.8 0.0 copy-done.1
  50.8 0.0 copy-start.2
  50.8 0.0 copy-start.3
  50.8 0.1 shard_map.119
  50.9 0.1 collective-permute-done.theirs_ref
  51.0 0.6 copy-done.2
  51.5 0.0 copy-done.3
  51.6 8.3 %shard_map.121 = (bf16[128,1024]{1,0:T(8,128)(2,1)}, bf16[128,128]{1,0:T(8,128)(2,1)}, bf16[128,128]{1,0:T(8,128)(2,1)}, bf16[2048,128]{1,0:T(8,128)(2,1)S(1)}, bf16[2048,128]{1,0:T(8,128)(2,1)S(1)}) custom-call(s32[1,1]{1,0:T(1,128)} %bitcast.8.seen_ref, bf16[1024,128]{1,0:T(8,128)(2,1)S(1)} %get-tuple-element.14.q_ref, ...), custom_call_target="tpu_custom_call" | custom-call | tf_op jit(solution)/shard_map/pallas_call | solution.py:247
  59.9 1.9 %collective-permute-start.1 = (bf16[2048,128]{1,0:T(8,128)(2,1)S(1)}, bf16[2048,128]{1,0:T(8,128)(2,1)S(1)}, u32[]{:S(2)}, u32[]{:S(2)}) collective-permute-start(bf16[2048,128]{1,0:T(8,128)(2,1)S(1)} %get-tuple-element.20), channel_id=1, source_target_pairs={{0,1},{1,0},{2,3},{3,2},{4,5},{5,4},{6,7},{7,6},{8,9},{9,8},{10,11... | collective-permute-start | bytes 1572872 | tf_op jit(solution)/shard_map/ppermute | solution.py:282
  61.8 1.9 %collective-permute-done.1 = bf16[2048,128]{1,0:T(8,128)(2,1)S(1)} collective-permute-done((bf16[2048,128]{1,0:T(8,128)(2,1)S(1)}, bf16[2048,128]{1,0:T(8,128)(2,1)S(1)}, u32[]{:S(2)}, u32[]{:S(2)}) %collective-permute-start.1) | collective-permute-done | bytes 524320 | tf_op jit(solution)/shard_map/ppermute | solution.py:282
  63.6 0.1 fusion
  63.8 29.4 %all_to_all.23 = bf16[256,8,128]{2,1,0:T(8,128)(2,1)S(1)} all-to-all(bf16[256,8,128]{2,1,0:T(8,128)(2,1)S(1)} %fusion), channel_id=1, replica_groups=mesh['head'=8,'x'=4,'y'=8,'core'=2] {'head','x','y'}, dimensions={0} | all-to-all | bytes 1048576 | tf_op jit(solution)/shard_map/all_to_all | solution.py:303
  93.1 0.7 shard_map.122
Async XLA Ops:
  2.2 48.6 %copy-start = (bf16[128,1024]{1,0:T(8,128)(2,1)S(1)}, bf16[128,1024]{1,0:T(8,128)(2,1)}, u32[]{:S(2)}) copy-start(bf16[128,1024]{1,0:T(8,128)(2,1)} %q_ref.1) | copy-start | bytes 786436
  2.2 48.6 %copy-start.1 = (bf16[128,1024]{1,0:T(8,128)(2,1)S(1)}, bf16[128,1024]{1,0:T(8,128)(2,1)}, u32[]{:S(2)}) copy-start(bf16[128,1024]{1,0:T(8,128)(2,1)} %g_ref.1) | copy-start | bytes 786436
  44.9 6.1 %collective-permute-start = (bf16[2048,128]{1,0:T(8,128)(2,1)S(1)}, bf16[2048,128]{1,0:T(8,128)(2,1)S(1)}, u32[]{:S(2)}, u32[]{:S(2)}) collective-permute-start(bf16[2048,128]{1,0:T(8,128)(2,1)S(1)} %bitcast.9), channel_id=1, source_target_pairs={{0,1},{1,0},{2,3},{3,2},{4,5},{5,4},{6,7},{7,6},{8,9},{9,8},{10,11... | collective-permute-start | bytes 1572872 | tf_op jit(solution)/shard_map/ppermute | solution.py:282
  50.8 0.8 copy-start.2
  50.8 0.8 copy-start.3
  59.9 3.8 %collective-permute-start.1 = (bf16[2048,128]{1,0:T(8,128)(2,1)S(1)}, bf16[2048,128]{1,0:T(8,128)(2,1)S(1)}, u32[]{:S(2)}, u32[]{:S(2)}) collective-permute-start(bf16[2048,128]{1,0:T(8,128)(2,1)S(1)} %get-tuple-element.20), channel_id=1, source_target_pairs={{0,1},{1,0},{2,3},{3,2},{4,5},{5,4},{6,7},{7,6},{8,9},{9,8},{10,11... | collective-permute-start | bytes 1572872 | tf_op jit(solution)/shard_map/ppermute | solution.py:282

commit v3 on v2

--- a/solution.py
+++ b/solution.py
@@ -295,6 +295,7 @@
     )(prefix_keys, prefix_values)
     mine = lax.all_to_all(messages, wide, 0, 0, tiled=True)
     q, g = stack_call(lengths, queries, cotangent)
+    mine, q, g = lax.optimization_barrier((mine, q, g))
     theirs = swap_cores(mine)
     dq, dok, dov, dmine, dtheirs = grad_call(
         seen, q, g, own_keys, own_values, mine, theirs

time: 94.3 us -> 93.5 us (level)
  blocking collectives: 72 us -> 29.1 us
  starting transfers between devices: 6.46 us -> 30.2 us
  waiting for transfers between devices: 1.93 us -> 20.9 us
    all_to_all x1 -> x0, blocking collectives: 42.7 us -> none  [per_device(): mine = lax.all_to_all(messages, wide, 0, 0, tiled=True)]
    all_to_all x0 -> x1, starting transfers between devices: none -> 23.3 us  [per_device(): mine = lax.all_to_all(messages, wide, 0, 0, tiled=True)]
    all_to_all x0 -> x1, waiting for transfers between devices: none -> 18.5 us  [per_device(): mine = lax.all_to_all(messages, wide, 0, 0, tiled=True)]
  transfers between devices with their start and end apart: 2 -> 3, of which waited for: 2 -> 3; matrix products, arithmetic and copies ran while one was open for 0% -> 0% of each run, Pallas kernels for 0% -> 0%
where the time goes in v3:
time: 93.5 us; the launch traced here: 93.1 us
  starting transfers between devices  30.2 us (32%)
  blocking collectives  29.1 us (31%)
  waiting for transfers between devices  20.9 us (22%)
  Pallas kernels  10.7 us (11%)
  between operations  1.99 us (2%)
    all_to_all x1, blocking collectives, per_device(): back = lax.all_to_all(summed, wide, 0, 0, tiled=True)  29.1 us
    all_to_all x1, starting transfers between devices, per_device(): mine = lax.all_to_all(messages, wide, 0, 0, tiled=True)  23.3 us
    all_to_all x1, waiting for transfers between devices, per_device(): mine = lax.all_to_all(messages, wide, 0, 0, tiled=True)  18.5 us
    pallas_call x1, Pallas kernels, grad_call(): pl.pallas_call(functools.partial(grad_kernel, core_axis='core', chunk=chu...  8.3 us
    ppermute x2, starting transfers between devices, swap_cores(): return lax.ppermute(block, 'core', [(0, 1), (1, 0)])  6.83 us
    ppermute x2, waiting for transfers between devices, swap_cores(): return lax.ppermute(block, 'core', [(0, 1), (1, 0)])  2.38 us
  transfers between devices with their start and end apart: 3, of which 3 were waited for; matrix products, arithmetic and copies ran while one was open for 0% of the time, Pallas kernels for 0%

profile of v3, /device:TPU:1, one launch (start us, length us, event | category | flops | bytes accessed | tf_op | source)
XLA Modules:
  0.0 93.1 jit_solution(9154051905391399700)
XLA Ops:
  0.6 1.6 %shard_map.119 = bf16[2048,128]{1,0:T(8,128)(2,1)} custom-call(bf16[4,1024]{1,0:T(4,128)(2,1)} %keys_ref.1, bf16[4,1024]{1,0:T(4,128)(2,1)} %values_ref.1), custom_call_target="tpu_custom_call" | custom-call | tf_op jit(solution)/shard_map/pallas_call | solution.py:289
  2.2 0.0 copy-start
  2.2 0.0 copy-start.1
  2.2 23.3 %all-to-all-start = ((bf16[256,8,128]{2,1,0:T(8,128)(2,1)}), bf16[256,8,128]{2,1,0:T(8,128)(2,1)S(1)}, u32[]{:S(2)}, u32[]{:S(2)}) async-start(bf16[256,8,128]{2,1,0:T(8,128)(2,1)} %bitcast.12), calls=%async_computation | async-start | bytes 1048576 | tf_op jit(solution)/shard_map/all_to_all | solution.py:296
  26.2 0.0 copy-done
  26.2 0.0 copy-done.1
  26.2 0.0 copy-start.2
  26.2 0.0 copy-start.3
  26.2 0.1 shard_map.120
  26.3 18.5 %all-to-all-done = bf16[256,8,128]{2,1,0:T(8,128)(2,1)S(1)} async-done(((bf16[256,8,128]{2,1,0:T(8,128)(2,1)}), bf16[256,8,128]{2,1,0:T(8,128)(2,1)S(1)}, u32[]{:S(2)}, u32[]{:S(2)}) %all-to-all-start) | async-done | bytes 524320 | tf_op jit(solution)/shard_map/all_to_all | solution.py:296
  44.9 4.6 %collective-permute-start = (bf16[2048,128]{1,0:T(8,128)(2,1)S(1)}, bf16[2048,128]{1,0:T(8,128)(2,1)S(1)}, u32[]{:S(2)}, u32[]{:S(2)}) collective-permute-start(bf16[2048,128]{1,0:T(8,128)(2,1)S(1)} %bitcast.9), channel_id=1, source_target_pairs={{0,1},{1,0},{2,3},{3,2},{4,5},{5,4},{6,7},{7,6},{8,9},{9,8},{10,11... | collective-permute-start | bytes 1572872 | tf_op jit(solution)/shard_map/ppermute | solution.py:282
  50.1 0.9 collective-permute-done.theirs_ref
  51.0 0.0 copy-done.2
  51.0 0.0 copy-done.3
  51.0 8.3 %shard_map.121 = (bf16[128,1024]{1,0:T(8,128)(2,1)}, bf16[128,128]{1,0:T(8,128)(2,1)}, bf16[128,128]{1,0:T(8,128)(2,1)}, bf16[2048,128]{1,0:T(8,128)(2,1)S(1)}, bf16[2048,128]{1,0:T(8,128)(2,1)S(1)}) custom-call(s32[1,1]{1,0:T(1,128)} %bitcast.8.seen_ref, bf16[1024,128]{1,0:T(8,128)(2,1)S(1)} %get-tuple-element.19.q_ref, ...), custom_call_target="tpu_custom_call" | custom-call | tf_op jit(solution)/shard_map/pallas_call | solution.py:247
  59.3 2.3 %collective-permute-start.1 = (bf16[2048,128]{1,0:T(8,128)(2,1)S(1)}, bf16[2048,128]{1,0:T(8,128)(2,1)S(1)}, u32[]{:S(2)}, u32[]{:S(2)}) collective-permute-start(bf16[2048,128]{1,0:T(8,128)(2,1)S(1)} %get-tuple-element.26), channel_id=1, source_target_pairs={{0,1},{1,0},{2,3},{3,2},{4,5},{5,4},{6,7},{7,6},{8,9},{9,8},{10,11... | collective-permute-start | bytes 1572872 | tf_op jit(solution)/shard_map/ppermute | solution.py:282
  61.6 1.5 %collective-permute-done.1 = bf16[2048,128]{1,0:T(8,128)(2,1)S(1)} collective-permute-done((bf16[2048,128]{1,0:T(8,128)(2,1)S(1)}, bf16[2048,128]{1,0:T(8,128)(2,1)S(1)}, u32[]{:S(2)}, u32[]{:S(2)}) %collective-permute-start.1) | collective-permute-done | bytes 524320 | tf_op jit(solution)/shard_map/ppermute | solution.py:282
  63.1 0.1 fusion
  63.2 29.1 %all_to_all.23 = bf16[256,8,128]{2,1,0:T(8,128)(2,1)S(1)} all-to-all(bf16[256,8,128]{2,1,0:T(8,128)(2,1)S(1)} %fusion), channel_id=1, replica_groups=mesh['head'=8,'x'=4,'y'=8,'core'=2] {'head','x','y'}, dimensions={0} | all-to-all | bytes 1048576 | tf_op jit(solution)/shard_map/all_to_all | solution.py:304
  92.4 0.7 shard_map.122
Async XLA Ops:
  2.2 24.0 %copy-start = (bf16[128,1024]{1,0:T(8,128)(2,1)S(1)}, bf16[128,1024]{1,0:T(8,128)(2,1)}, u32[]{:S(2)}) copy-start(bf16[128,1024]{1,0:T(8,128)(2,1)} %q_ref.1) | copy-start | bytes 786436
  2.2 24.0 %copy-start.1 = (bf16[128,1024]{1,0:T(8,128)(2,1)S(1)}, bf16[128,1024]{1,0:T(8,128)(2,1)}, u32[]{:S(2)}) copy-start(bf16[128,1024]{1,0:T(8,128)(2,1)} %g_ref.1) | copy-start | bytes 786436
  2.2 42.7 %all-to-all-start = ((bf16[256,8,128]{2,1,0:T(8,128)(2,1)}), bf16[256,8,128]{2,1,0:T(8,128)(2,1)S(1)}, u32[]{:S(2)}, u32[]{:S(2)}) async-start(bf16[256,8,128]{2,1,0:T(8,128)(2,1)} %bitcast.12), calls=%async_computation | async-start | bytes 1048576 | tf_op jit(solution)/shard_map/all_to_all | solution.py:296
  26.2 24.8 %copy-start.2 = (bf16[128,128]{1,0:T(8,128)(2,1)S(1)}, bf16[128,128]{1,0:T(8,128)(2,1)}, u32[]{:S(2)}) copy-start(bf16[128,128]{1,0:T(8,128)(2,1)} %own_k_ref.1) | copy-start | bytes 98308
  26.2 24.8 %copy-start.3 = (bf16[128,128]{1,0:T(8,128)(2,1)S(1)}, bf16[128,128]{1,0:T(8,128)(2,1)}, u32[]{:S(2)}) copy-start(bf16[128,128]{1,0:T(8,128)(2,1)} %own_v_ref.1) | copy-start | bytes 98308
  44.9 6.1 %collective-permute-start = (bf16[2048,128]{1,0:T(8,128)(2,1)S(1)}, bf16[2048,128]{1,0:T(8,128)(2,1)S(1)}, u32[]{:S(2)}, u32[]{:S(2)}) collective-permute-start(bf16[2048,128]{1,0:T(8,128)(2,1)S(1)} %bitcast.9), channel_id=1, source_target_pairs={{0,1},{1,0},{2,3},{3,2},{4,5},{5,4},{6,7},{7,6},{8,9},{9,8},{10,11... | collective-permute-start | bytes 1572872 | tf_op jit(solution)/shard_map/ppermute | solution.py:282
  59.3 3.8 %collective-permute-start.1 = (bf16[2048,128]{1,0:T(8,128)(2,1)S(1)}, bf16[2048,128]{1,0:T(8,128)(2,1)S(1)}, u32[]{:S(2)}, u32[]{:S(2)}) collective-permute-start(bf16[2048,128]{1,0:T(8,128)(2,1)S(1)} %get-tuple-element.26), channel_id=1, source_target_pairs={{0,1},{1,0},{2,3},{3,2},{4,5},{5,4},{6,7},{7,6},{8,9},{9,8},{10,11... | collective-permute-start | bytes 1572872 | tf_op jit(solution)/shard_map/ppermute | solution.py:282

commit v4 on v2

--- a/solution.py
+++ b/solution.py
@@ -14,6 +14,8 @@
 TILE = 8
 HALF = 4
 CORES = 2
+SPAN = 4
+STEP = 256
 VMEM = pl.BlockSpec(memory_space=pltpu.VMEM)
 
 
@@ -65,8 +67,13 @@
     return op(block.reshape(rows // TILE, TILE, lanes), axis=0)
 
 
-def stack_kernel(length_ref, q_ref, g_ref, q_out, g_out):
+def stack_kernel(
+    length_ref, seen_ref, q_ref, g_ref, k_ref, v_ref, q_out, g_out, seen_out, k_out, v_out
+):
     tokens = q_ref.shape[0]
+    k_out[...] = k_ref[...]
+    v_out[...] = v_ref[...]
+    seen_out[...] = jnp.broadcast_to(seen_ref[...], seen_out.shape)
     live = lax.broadcasted_iota(jnp.int32, (tokens, 128), 0) < length_ref[...]
     for head in range(q_ref.shape[1] // 128):
         rows = slice(head * tokens, (head + 1) * tokens)
@@ -75,15 +82,79 @@
         g_out[rows, :] = jnp.where(live, grad, 0.0).astype(BF16)
 
 
+def score_masks(seen, core, tokens, half, lanes):
+    inner = lax.broadcasted_iota(jnp.int32, (TILE, lanes), 0)
+    spread = (inner // HALF) * TILE + inner % HALF
+    room = (seen - spread - core * HALF, seen - spread - (1 - core) * HALF)
+
+    def hide(s, row, size):
+        if row == 0:
+            token = lax.broadcasted_iota(jnp.int32, (size, lanes), 1) % tokens
+            index = lax.broadcasted_iota(jnp.int32, (size, lanes), 0)
+            return jnp.where(index <= token, s, NEGATIVE)
+        block = (row - tokens) // half
+        local = row - tokens - block * half
+        if local + size <= half // 2:
+            return s
+        count = size // TILE
+        parts = s.reshape(count, TILE, lanes)
+        place = 2 * (local + TILE * lax.broadcasted_iota(jnp.int32, parts.shape, 0))
+        return jnp.where(place < room[block][None], parts, NEGATIVE).reshape(size, lanes)
+
+    return hide
+
+
+def early_kernel(
+    seen_ref,
+    q_ref,
+    own_k_ref,
+    own_v_ref,
+    mine_ref,
+    k_ref,
+    v_ref,
+    kt_ref,
+    s_ref,
+    peak_ref,
+    *,
+    core_axis,
+    chunk,
+    span,
+):
+    tokens = own_k_ref.shape[0]
+    half = mine_ref.shape[0] // 2
+    kept = tokens + half
+    k_ref[0:tokens, :] = own_k_ref[...]
+    v_ref[0:tokens, :] = own_v_ref[...]
+    kt_ref[:, 0:tokens] = own_k_ref[...].astype(F32).T.astype(BF16)
+    for at in range(0, half, STEP):
+        keys, values = split_messages(mine_ref[2 * at : 2 * (at + STEP), :])
+        row = tokens + at
+        k_ref[row : row + STEP, :] = keys
+        v_ref[row : row + STEP, :] = values
+        kt_ref[:, row : row + STEP] = keys.astype(F32).T.astype(BF16)
+    lanes = span * tokens
+    hide = score_masks(seen_ref[...], lax.axis_index(core_axis), tokens, half, lanes)
+    for pair in range(q_ref.shape[0] // lanes):
+        rows = slice(pair * lanes, (pair + 1) * lanes)
+        q = q_ref[rows, :]
+        peak = jnp.full((TILE, lanes), NEGATIVE, F32)
+        for row, size in [(0, tokens)] + [(row, chunk) for row in range(tokens, kept, chunk)]:
+            s = hide(dot(k_ref[row : row + size, :], q, NT), row, size)
+            s_ref[row : row + size, rows] = s
+            peak = jnp.maximum(peak, fold(s, jnp.max))
+        peak_ref[:, rows] = peak
+
+
 def grad_kernel(
     seen_ref,
     q_ref,
     g_ref,
-    own_k_ref,
-    own_v_ref,
-    mine_ref,
+    v_ref,
+    kt_ref,
+    s_ref,
+    peak_ref,
     theirs_ref,
-    dq_ref,
+    dqt_ref,
     dok_ref,
     dov_ref,
     dmine_ref,
@@ -100,46 +171,24 @@
     chunk,
     span,
 ):
-    tokens = own_k_ref.shape[0]
+    half = theirs_ref.shape[0] // 2
+    kept = v_ref.shape[0]
+    tokens = kept - half
     group = q_ref.shape[0] // tokens
-    half = mine_ref.shape[0] // 2
     key_count = tokens + 2 * half
     factor = 128 ** (-0.5)
     scale = factor * math.log2(math.e)
-    core = lax.axis_index(core_axis)
-
-    k_s[0:tokens, :] = own_k_ref[...]
-    v_s[0:tokens, :] = own_v_ref[...]
-    kt_s[:, 0:tokens] = own_k_ref[...].astype(F32).T.astype(BF16)
-    step = 256
-    for block, ref in enumerate((mine_ref, theirs_ref)):
-        for at in range(0, half, step):
-            keys, values = split_messages(ref[2 * at : 2 * (at + step), :])
-            row = tokens + block * half + at
-            k_s[row : row + step, :] = keys
-            v_s[row : row + step, :] = values
-            kt_s[:, row : row + step] = keys.astype(F32).T.astype(BF16)
+    step = STEP
+    for at in range(0, half, step):
+        keys, values = split_messages(theirs_ref[2 * at : 2 * (at + step), :])
+        k_s[at : at + step, :] = keys
+        v_s[at : at + step, :] = values
+        kt_s[:, at : at + step] = keys.astype(F32).T.astype(BF16)
 
     lanes = span * tokens
-    starts = [(0, tokens)] + [(row, chunk) for row in range(tokens, key_count, chunk)]
-    inner = lax.broadcasted_iota(jnp.int32, (TILE, lanes), 0)
-    spread = (inner // HALF) * TILE + inner % HALF
-    seen = jnp.broadcast_to(seen_ref[...], (TILE, lanes))
-    room = (seen - spread - core * HALF, seen - spread - (1 - core) * HALF)
-
-    def hide(s, row, size):
-        if row == 0:
-            token = lax.broadcasted_iota(jnp.int32, (size, lanes), 1) % tokens
-            index = lax.broadcasted_iota(jnp.int32, (size, lanes), 0)
-            return jnp.where(index <= token, s, NEGATIVE)
-        block = (row - tokens) // half
-        local = row - tokens - block * half
-        if local + size <= half // 2:
-            return s
-        count = size // TILE
-        parts = s.reshape(count, TILE, lanes)
-        place = 2 * (local + TILE * lax.broadcasted_iota(jnp.int32, parts.shape, 0))
-        return jnp.where(place < room[block][None], parts, NEGATIVE).reshape(size, lanes)
+    late = [(row, chunk) for row in range(kept, key_count, chunk)]
+    starts = [(0, tokens)] + [(row, chunk) for row in range(tokens, kept, chunk)] + late
+    hide = score_masks(seen_ref[...], lax.axis_index(core_axis), tokens, half, lanes)
 
     pairs = group // span
 
@@ -150,13 +199,14 @@
             self.rows = rows
             self.w, self.p = w_s.at[pair % 2], p_s.at[pair % 2]
             self.q, self.g = q_ref[rows, :], g_ref[rows, :]
-            self.peak = jnp.full((TILE, lanes), NEGATIVE, F32)
+            self.peak = peak_ref[:, rows]
             self.total = jnp.zeros((TILE, lanes), F32)
             self.weighted = jnp.zeros((TILE, lanes), F32)
             self.dqt = jnp.zeros((128, lanes), F32)
 
         def score(self, row, size):
-            s = hide(dot(k_s[row : row + size, :], self.q, NT), row, size)
+            keys = k_s[row - kept : row - kept + size, :]
+            s = hide(dot(keys, self.q, NT), row, size)
             self.w[row : row + size, :] = s
             self.peak = jnp.maximum(self.peak, fold(s, jnp.max))
 
@@ -164,8 +214,14 @@
             self.peak = jnp.max(self.peak, axis=0, keepdims=True)
 
         def weigh(self, row, size):
-            gp = dot(v_s[row : row + size, :], self.g, NT)
-            w = jnp.exp2((self.w[row : row + size, :] - self.peak) * scale)
+            if row < kept:
+                values = v_ref[row : row + size, :]
+                s = s_ref[row : row + size, self.rows]
+            else:
+                values = v_s[row - kept : row - kept + size, :]
+                s = self.w[row : row + size, :]
+            gp = dot(values, self.g, NT)
+            w = jnp.exp2((s - self.peak) * scale)
             self.w[row : row + size, :] = w
             self.p[row : row + size, :] = gp
             self.total = self.total + fold(w, jnp.sum)
@@ -180,7 +236,11 @@
             grads = probs * (self.p[row : row + size, :] - self.delta)
             probs = probs.astype(BF16)
             grads = grads.astype(BF16)
-            self.dqt = self.dqt + dot(kt_s[:, row : row + size], grads, NN)
+            if row < kept:
+                keys = kt_ref[:, row : row + size]
+            else:
+                keys = kt_s[:, row - kept : row - kept + size]
+            self.dqt = self.dqt + dot(keys, grads, NN)
             dk = dot(grads, self.q, NN)
             dv = dot(probs, self.g, NN)
             if self.pair == 0:
@@ -191,17 +251,13 @@
                 dv_s[row : row + size, :] += dv
 
         def finish(self):
-            dqt = self.dqt * factor
-            for sub in range(span):
-                head = self.pair * span + sub
-                block = dqt[:, sub * tokens : (sub + 1) * tokens].T.astype(BF16)
-                dq_ref[:, head * 128 : (head + 1) * 128] = block
+            dqt_ref[:, self.rows] = self.dqt
 
     done = None
     for pair in range(pairs + 1):
         work = Block(pair) if pair < pairs else None
         if work:
-            for at in starts:
+            for at in late:
                 work.score(*at)
             work.top()
         for at in starts:
@@ -215,8 +271,8 @@
             done.finish()
         done = work
 
-    dok_ref[...] = (dk_s[0:tokens, :] * factor).astype(BF16)
-    dov_ref[...] = dv_s[0:tokens, :].astype(BF16)
+    dok_ref[...] = dk_s[0:tokens, :]
+    dov_ref[...] = dv_s[0:tokens, :]
     for block, ref in enumerate((dmine_ref, dtheirs_ref)):
         for at in range(0, half, step):
             row = tokens + block * half + at
@@ -229,43 +285,91 @@
     return pltpu.CompilerParams(vmem_limit_bytes=count * 1024 * 1024)
 
 
-def stack_call(lengths, queries, cotangent):
+def stack_call(lengths, seen, queries, cotangent, own_keys, own_values):
     tokens, width = queries.shape
+    stacked = jax.ShapeDtypeStruct((tokens * (width // 128), 128), BF16)
     return pl.pallas_call(
         stack_kernel,
-        out_shape=(jax.ShapeDtypeStruct((tokens * (width // 128), 128), BF16),) * 2,
-        in_specs=[VMEM] * 3,
-        out_specs=(VMEM,) * 2,
+        out_shape=(
+            stacked,
+            stacked,
+            jax.ShapeDtypeStruct((TILE, SPAN * tokens), jnp.int32),
+            jax.ShapeDtypeStruct(own_keys.shape, BF16),
+            jax.ShapeDtypeStruct(own_values.shape, BF16),
+        ),
+        in_specs=[VMEM] * 6,
+        out_specs=(VMEM,) * 5,
         compiler_params=megabytes(4),
-    )(lengths.reshape(1, 1), queries, cotangent)
-
-
-def grad_call(seen, q, g, own_keys, own_values, mine, theirs, chunk=512, span=4):
-    tokens = own_keys.shape[0]
+    )(lengths.reshape(1, 1), seen.reshape(1, 1), queries, cotangent, own_keys, own_values)
+
+
+def early_call(seen, q, own_keys, own_values, mine, chunk=512, span=SPAN):
+    kept = own_keys.shape[0] + mine.shape[0] // 2
+    return pl.pallas_call(
+        functools.partial(early_kernel, core_axis="core", chunk=chunk, span=span),
+        out_shape=(
+            jax.ShapeDtypeStruct((kept, 128), BF16),
+            jax.ShapeDtypeStruct((kept, 128), BF16),
+            jax.ShapeDtypeStruct((128, kept), BF16),
+            jax.ShapeDtypeStruct((kept, q.shape[0]), F32),
+            jax.ShapeDtypeStruct((TILE, q.shape[0]), F32),
+        ),
+        in_specs=[VMEM] * 5,
+        out_specs=(VMEM,) * 5,
+        compiler_params=megabytes(8),
+    )(seen, q, own_keys, own_values, mine)
+
+
+def grad_call(seen, q, g, values, keys_t, scores, peak, theirs, tokens, chunk=512, span=SPAN):
     stacked = q.shape[0]
-    key_count = tokens + mine.shape[0]
+    half = theirs.shape[0] // 2
+    key_count = tokens + 2 * half
     return pl.pallas_call(
         functools.partial(grad_kernel, core_axis="core", chunk=chunk, span=span),
         out_shape=(
-            jax.ShapeDtypeStruct((tokens, stacked // tokens * 128), BF16),
-            jax.ShapeDtypeStruct(own_keys.shape, BF16),
-            jax.ShapeDtypeStruct(own_values.shape, BF16),
-            jax.ShapeDtypeStruct(mine.shape, BF16),
+            jax.ShapeDtypeStruct((128, stacked), F32),
+            jax.ShapeDtypeStruct((tokens, 128), F32),
+            jax.ShapeDtypeStruct((tokens, 128), F32),
             jax.ShapeDtypeStruct(theirs.shape, BF16),
-        ),
-        in_specs=[VMEM] * 7,
+            jax.ShapeDtypeStruct(theirs.shape, BF16),
+        ),
+        in_specs=[VMEM] * 8,
         out_specs=(VMEM,) * 5,
         scratch_shapes=[
-            pltpu.VMEM((key_count, 128), BF16),
-            pltpu.VMEM((key_count, 128), BF16),
-            pltpu.VMEM((128, key_count), BF16),
+            pltpu.VMEM((half, 128), BF16),
+            pltpu.VMEM((half, 128), BF16),
+            pltpu.VMEM((128, half), BF16),
             pltpu.VMEM((2, key_count, span * tokens), F32),
             pltpu.VMEM((2, key_count, span * tokens), F32),
             pltpu.VMEM((key_count, 128), F32),
             pltpu.VMEM((key_count, 128), F32),
         ],
-        compiler_params=megabytes(40),
-    )(seen.reshape(1, 1), q, g, own_keys, own_values, mine, theirs)
+        compiler_params=megabytes(36),
+    )(seen, q, g, values, keys_t, scores, peak, theirs)
+
+
+def finish_kernel(dqt_ref, dk_ref, dv_ref, dq_ref, dok_ref, dov_ref):
+    factor = 128 ** (-0.5)
+    tokens = dk_ref.shape[0]
+    for head in range(dq_ref.shape[1] // 128):
+        block = dqt_ref[:, head * tokens : (head + 1) * tokens] * factor
+        dq_ref[:, head * 128 : (head + 1) * 128] = block.T.astype(BF16)
+    dok_ref[...] = (dk_ref[...] * factor).astype(BF16)
+    dov_ref[...] = dv_ref[...].astype(BF16)
+
+
+def finish_call(dqt, dk, dv, shape):
+    return pl.pallas_call(
+        finish_kernel,
+        out_shape=(
+            jax.ShapeDtypeStruct(shape, BF16),
+            jax.ShapeDtypeStruct(dk.shape, BF16),
+            jax.ShapeDtypeStruct(dv.shape, BF16),
+        ),
+        in_specs=[VMEM] * 3,
+        out_specs=(VMEM,) * 3,
+        compiler_params=megabytes(8),
+    )(dqt, dk, dv)
 
 
 def sum_kernel(in_ref, keys_ref, values_ref):
@@ -294,13 +398,16 @@
         scratch_shapes=[pltpu.VMEM((TILE, prefix_keys.shape[1]), F32)],
     )(prefix_keys, prefix_values)
     mine = lax.all_to_all(messages, wide, 0, 0, tiled=True)
-    q, g = stack_call(lengths, queries, cotangent)
+    staged = stack_call(lengths, seen, queries, cotangent, own_keys, own_values)
+    mine, staged = lax.optimization_barrier((mine, staged))
     theirs = swap_cores(mine)
-    dq, dok, dov, dmine, dtheirs = grad_call(
-        seen, q, g, own_keys, own_values, mine, theirs
-    )
+    q, g, seen, held_keys, held_values = staged
+    early = early_call(seen, q, held_keys, held_values, mine)
+    dqt, dk, dv, dmine, dtheirs = grad_call(seen, q, g, *early[1:], theirs, own_keys.shape[0])
     summed = (dmine.astype(F32) + swap_cores(dtheirs).astype(F32)).astype(BF16)
+    summed, dqt, dk, dv = lax.optimization_barrier((summed, dqt, dk, dv))
     back = lax.all_to_all(summed, wide, 0, 0, tiled=True)
+    dq, dok, dov = finish_call(dqt, dk, dv, queries.shape)
     dkeys, dvalues = pl.pallas_call(
         sum_kernel,
         out_shape=(jax.ShapeDtypeStruct(prefix_keys.shape, F32),) * 2,

time: 94.3 us -> 93.1 us (0.987)
  blocking collectives: 72 us -> 0 us
  waiting for transfers between devices: 1.93 us -> 35.5 us
  starting transfers between devices: 6.46 us -> 39.4 us
  local copies, waits for them, and re-layouts: 0.59 us -> 3.41 us
    all_to_all x2 -> x0, blocking collectives: 72 us -> none  [the longest x1 42.7 us: per_device(): mine = lax.all_to_all(messages, wide, 0, 0, tiled=True)]
    all_to_all x0 -> x2, waiting for transfers between devices: none -> 33.8 us  [the longest x1 19.3 us: per_device(): back = lax.all_to_all(summed, wide, 0, 0, tiled=True)]
    all_to_all x0 -> x2, starting transfers between devices: none -> 32.5 us  [the longest x1 23.2 us: per_device(): mine = lax.all_to_all(messages, wide, 0, 0, tiled=True)]
    unnamed x8, local copies, waits for them, and re-layouts: 0.59 us -> 3.41 us
    pallas_call x1 -> x3, Pallas kernels: 0.12 us -> 2.26 us  [the longest x1 1.3 us: early_call(): pl.pallas_call(functools.partial(early_kernel, core_axis='core', chunk=ch...]
    pallas_call x1, Pallas kernels: 8.3 us -> 6.82 us  [grad_call(): pl.pallas_call(functools.partial(grad_kernel, core_axis='core', chunk=chu...]
  transfers between devices with their start and end apart: 2 -> 4, of which waited for: 2 -> 4; matrix products, arithmetic and copies ran while one was open for 0% -> 0% of each run, Pallas kernels for 0% -> 2%
where the time goes in v4:
time: 93.1 us; the launch traced here: 92.6 us
  starting transfers between devices  39.4 us (42%)
  waiting for transfers between devices  35.5 us (38%)
  Pallas kernels  11.3 us (12%)
  local copies, waits for them, and re-layouts  3.41 us (4%)
  between operations  1.98 us (2%)
    all_to_all x1, starting transfers between devices, per_device(): mine = lax.all_to_all(messages, wide, 0, 0, tiled=True)  23.2 us
    all_to_all x1, waiting for transfers between devices, per_device(): back = lax.all_to_all(summed, wide, 0, 0, tiled=True)  19.3 us
    all_to_all x1, waiting for transfers between devices, per_device(): mine = lax.all_to_all(messages, wide, 0, 0, tiled=True)  14.5 us
    all_to_all x1, starting transfers between devices, per_device(): back = lax.all_to_all(summed, wide, 0, 0, tiled=True)  9.34 us
    ppermute x2, starting transfers between devices, swap_cores(): return lax.ppermute(block, 'core', [(0, 1), (1, 0)])  6.84 us
    pallas_call x1, Pallas kernels, grad_call(): pl.pallas_call(functools.partial(grad_kernel, core_axis='core', chunk=chu...  6.82 us
    unnamed x8, local copies, waits for them, and re-layouts  3.41 us
  transfers between devices with their start and end apart: 4, of which 4 were waited for; matrix products, arithmetic and copies ran while one was open for 0% of the time, Pallas kernels for 2%

profile of v4, /device:TPU:1, one launch (start us, length us, event | category | flops | bytes accessed | tf_op | source)
XLA Modules:
  0.0 92.6 jit_solution(2985770174769561768)
XLA Ops:
  0.6 1.6 %shard_map.119 = bf16[2048,128]{1,0:T(8,128)(2,1)} custom-call(bf16[4,1024]{1,0:T(4,128)(2,1)} %keys_ref.1, bf16[4,1024]{1,0:T(4,128)(2,1)} %values_ref.1), custom_call_target="tpu_custom_call" | custom-call | tf_op jit(solution)/shard_map/pallas_call | solution.py:393
  2.2 23.2 %all-to-all-start = ((bf16[256,8,128]{2,1,0:T(8,128)(2,1)}), bf16[256,8,128]{2,1,0:T(8,128)(2,1)S(1)}, u32[]{:S(2)}, u32[]{:S(2)}) async-start(bf16[256,8,128]{2,1,0:T(8,128)(2,1)} %bitcast.11), calls=%async_computation | async-start | bytes 1048576 | tf_op jit(solution)/shard_map/all_to_all | solution.py:400
  26.7 0.0 copy-start
  26.7 0.9 %copy-done = bf16[128,1024]{1,0:T(8,128)(2,1)S(1)} copy-done((bf16[128,1024]{1,0:T(8,128)(2,1)S(1)}, bf16[128,1024]{1,0:T(8,128)(2,1)}, u32[]{:S(2)}) %copy-start) | copy-done | bytes 262168
  27.6 0.0 copy-start.1
  27.6 0.9 %copy-done.1 = bf16[128,1024]{1,0:T(8,128)(2,1)S(1)} copy-done((bf16[128,1024]{1,0:T(8,128)(2,1)S(1)}, bf16[128,1024]{1,0:T(8,128)(2,1)}, u32[]{:S(2)}) %copy-start.1) | copy-done | bytes 262168
  28.6 0.0 copy-start.2
  28.6 0.8 copy-done.2
  29.3 0.0 copy-start.3
  29.3 0.8 copy-done.3
  30.1 0.1 shard_map.120
  30.2 14.5 %all-to-all-done = bf16[256,8,128]{2,1,0:T(8,128)(2,1)S(1)} async-done(((bf16[256,8,128]{2,1,0:T(8,128)(2,1)}), bf16[256,8,128]{2,1,0:T(8,128)(2,1)S(1)}, u32[]{:S(2)}, u32[]{:S(2)}) %all-to-all-start) | async-done | bytes 524320 | tf_op jit(solution)/shard_map/all_to_all | solution.py:400
  44.8 4.6 %collective-permute-start = (bf16[2048,128]{1,0:T(8,128)(2,1)S(1)}, bf16[2048,128]{1,0:T(8,128)(2,1)S(1)}, u32[]{:S(2)}, u32[]{:S(2)}) collective-permute-start(bf16[2048,128]{1,0:T(8,128)(2,1)S(1)} %bitcast.8), channel_id=1, source_target_pairs={{0,1},{1,0},{2,3},{3,2},{4,5},{5,4},{6,7},{7,6},{8,9},{9,8},{10,11... | collective-permute-start | bytes 1572872 | tf_op jit(solution)/shard_map/ppermute | solution.py:386
  49.3 1.3 %shard_map.121 = (bf16[1152,128]{1,0:T(8,128)(2,1)}, bf16[1152,128]{1,0:T(8,128)(2,1)S(1)}, bf16[128,1152]{1,0:T(8,128)(2,1)S(1)}, f32[1152,1024]{1,0:T(8,128)S(1)}, f32[8,1024]{1,0:T(8,128)S(1)}) custom-call(s32[8,512]{1,0:T(8,128)S(1)} %get-tuple-element.39.seen_ref, bf16[1024,128]{1,0:T(8,128)(2,1)S(1)} %get-tuple-element.40.q_ref, ...), custom_call_target="tpu_custom_call" | custom-call | tf_op jit(solution)/shard_map/pallas_call | solution.py:308
  50.6 0.2 collective-permute-done.theirs_ref
  50.8 6.8 %shard_map.122 = (f32[128,1024]{1,0:T(8,128)S(1)}, f32[128,128]{1,0:T(8,128)S(1)}, f32[128,128]{1,0:T(8,128)S(1)}, bf16[2048,128]{1,0:T(8,128)(2,1)S(1)}, bf16[2048,128]{1,0:T(8,128)(2,1)S(1)}) custom-call(s32[8,512]{1,0:T(8,128)S(1)} %get-tuple-element.39.seen_ref, bf16[1024,128]{1,0:T(8,128)(2,1)S(1)} %get-tuple-element.40.q_ref, ...), custom_call_target="tpu_custom_call" | custom-call | tf_op jit(solution)/shard_map/pallas_call | solution.py:327
  57.7 2.3 %collective-permute-start.1 = (bf16[2048,128]{1,0:T(8,128)(2,1)S(1)}, bf16[2048,128]{1,0:T(8,128)(2,1)S(1)}, u32[]{:S(2)}, u32[]{:S(2)}) collective-permute-start(bf16[2048,128]{1,0:T(8,128)(2,1)S(1)} %get-tuple-element.50), channel_id=1, source_target_pairs={{0,1},{1,0},{2,3},{3,2},{4,5},{5,4},{6,7},{7,6},{8,9},{9,8},{10,11... | collective-permute-start | bytes 1572872 | tf_op jit(solution)/shard_map/ppermute | solution.py:386
  60.0 1.5 %collective-permute-done.1 = bf16[2048,128]{1,0:T(8,128)(2,1)S(1)} collective-permute-done((bf16[2048,128]{1,0:T(8,128)(2,1)S(1)}, bf16[2048,128]{1,0:T(8,128)(2,1)S(1)}, u32[]{:S(2)}, u32[]{:S(2)}) %collective-permute-start.1) | collective-permute-done | bytes 524320 | tf_op jit(solution)/shard_map/ppermute | solution.py:386
  61.5 0.9 %add_convert_fusion = bf16[2048,128]{1,0:T(8,128)(2,1)} fusion(bf16[2048,128]{1,0:T(8,128)(2,1)S(1)} %collective-permute-done.1, bf16[2048,128]{1,0:T(8,128)(2,1)S(1)} %get-tuple-element.49), kind=kLoop, calls=%fused_computation | loop fusion | flops 1048576 | bytes 1572864 | tf_op jit(solution)/shard_map/convert_element_type | solution.py:407
  62.4 9.3 %all-to-all-start.1 = ((bf16[256,8,128]{2,1,0:T(8,128)(2,1)}), bf16[256,8,128]{2,1,0:T(8,128)(2,1)S(1)}, u32[]{:S(2)}, u32[]{:S(2)}) async-start(bf16[256,8,128]{2,1,0:T(8,128)(2,1)} %bitcast.4), calls=%async_computation.1 | async-start | bytes 1048576 | tf_op jit(solution)/shard_map/all_to_all | solution.py:409
  71.8 0.8 shard_map.123
  72.6 19.3 %all-to-all-done.1 = bf16[256,8,128]{2,1,0:T(8,128)(2,1)S(1)} async-done(((bf16[256,8,128]{2,1,0:T(8,128)(2,1)}), bf16[256,8,128]{2,1,0:T(8,128)(2,1)S(1)}, u32[]{:S(2)}, u32[]{:S(2)}) %all-to-all-start.1) | async-done | bytes 524320 | tf_op jit(solution)/shard_map/all_to_all | solution.py:409
  91.9 0.7 shard_map.124
Async XLA Ops:
  2.2 42.6 %all-to-all-start = ((bf16[256,8,128]{2,1,0:T(8,128)(2,1)}), bf16[256,8,128]{2,1,0:T(8,128)(2,1)S(1)}, u32[]{:S(2)}, u32[]{:S(2)}) async-start(bf16[256,8,128]{2,1,0:T(8,128)(2,1)} %bitcast.11), calls=%async_computation | async-start | bytes 1048576 | tf_op jit(solution)/shard_map/all_to_all | solution.py:400
  26.7 1.0 %copy-start = (bf16[128,1024]{1,0:T(8,128)(2,1)S(1)}, bf16[128,1024]{1,0:T(8,128)(2,1)}, u32[]{:S(2)}) copy-start(bf16[128,1024]{1,0:T(8,128)(2,1)} %q_ref.1) | copy-start | bytes 786436
  27.6 0.9 %copy-start.1 = (bf16[128,1024]{1,0:T(8,128)(2,1)S(1)}, bf16[128,1024]{1,0:T(8,128)(2,1)}, u32[]{:S(2)}) copy-start(bf16[128,1024]{1,0:T(8,128)(2,1)} %g_ref.1) | copy-start | bytes 786436
  28.6 0.8 copy-start.2
  29.3 0.8 copy-start.3
  44.8 6.1 %collective-permute-start = (bf16[2048,128]{1,0:T(8,128)(2,1)S(1)}, bf16[2048,128]{1,0:T(8,128)(2,1)S(1)}, u32[]{:S(2)}, u32[]{:S(2)}) collective-permute-start(bf16[2048,128]{1,0:T(8,128)(2,1)S(1)} %bitcast.8), channel_id=1, source_target_pairs={{0,1},{1,0},{2,3},{3,2},{4,5},{5,4},{6,7},{7,6},{8,9},{9,8},{10,11... | collective-permute-start | bytes 1572872 | tf_op jit(solution)/shard_map/ppermute | solution.py:386
  57.7 3.8 %collective-permute-start.1 = (bf16[2048,128]{1,0:T(8,128)(2,1)S(1)}, bf16[2048,128]{1,0:T(8,128)(2,1)S(1)}, u32[]{:S(2)}, u32[]{:S(2)}) collective-permute-start(bf16[2048,128]{1,0:T(8,128)(2,1)S(1)} %get-tuple-element.50), channel_id=1, source_target_pairs={{0,1},{1,0},{2,3},{3,2},{4,5},{5,4},{6,7},{7,6},{8,9},{9,8},{10,11... | collective-permute-start | bytes 1572872 | tf_op jit(solution)/shard_map/ppermute | solution.py:386
  62.4 29.5 %all-to-all-start.1 = ((bf16[256,8,128]{2,1,0:T(8,128)(2,1)}), bf16[256,8,128]{2,1,0:T(8,128)(2,1)S(1)}, u32[]{:S(2)}, u32[]{:S(2)}) async-start(bf16[256,8,128]{2,1,0:T(8,128)(2,1)} %bitcast.4), calls=%async_computation.1 | async-start | bytes 1048576 | tf_op jit(solution)/shard_map/all_to_all | solution.py:409

commit v5 on v4

--- a/solution.py
+++ b/solution.py
@@ -404,10 +404,10 @@
     q, g, seen, held_keys, held_values = staged
     early = early_call(seen, q, held_keys, held_values, mine)
     dqt, dk, dv, dmine, dtheirs = grad_call(seen, q, g, *early[1:], theirs, own_keys.shape[0])
-    summed = (dmine.astype(F32) + swap_cores(dtheirs).astype(F32)).astype(BF16)
-    summed, dqt, dk, dv = lax.optimization_barrier((summed, dqt, dk, dv))
+    dq, dok, dov = finish_call(dqt, dk, dv, queries.shape)
+    arrived, dok = lax.optimization_barrier((swap_cores(dtheirs), dok))
+    summed = (dmine.astype(F32) + arrived.astype(F32)).astype(BF16)
     back = lax.all_to_all(summed, wide, 0, 0, tiled=True)
-    dq, dok, dov = finish_call(dqt, dk, dv, queries.shape)
     dkeys, dvalues = pl.pallas_call(
         sum_kernel,
         out_shape=(jax.ShapeDtypeStruct(prefix_keys.shape, F32),) * 2,

time: 93.1 us -> 92 us (0.988)
  blocking collectives: 0 us -> 29.2 us
  waiting for transfers between devices: 35.5 us -> 15.4 us
  starting transfers between devices: 39.4 us -> 30 us
    all_to_all x0 -> x1, blocking collectives: none -> 29.2 us  [per_device(): back = lax.all_to_all(summed, wide, 0, 0, tiled=True)]
    all_to_all x1 -> x0, waiting for transfers between devices: 19.3 us -> none  [per_device(): back = lax.all_to_all(summed, wide, 0, 0, tiled=True)]
    all_to_all x1 -> x0, starting transfers between devices: 9.34 us -> none  [per_device(): back = lax.all_to_all(summed, wide, 0, 0, tiled=True)]
  transfers between devices with their start and end apart: 4 -> 3, of which waited for: 4 -> 3; matrix products, arithmetic and copies ran while one was open for 0% -> 0% of each run, Pallas kernels for 2% -> 2%
where the time goes in v5:
time: 92 us; the launch traced here: 91.5 us
  starting transfers between devices  30 us (33%)
  blocking collectives  29.2 us (32%)
  waiting for transfers between devices  15.4 us (17%)
  Pallas kernels  11.4 us (12%)
  local copies, waits for them, and re-layouts  3.41 us (4%)
  between operations  1.98 us (2%)
    all_to_all x1, blocking collectives, per_device(): back = lax.all_to_all(summed, wide, 0, 0, tiled=True)  29.2 us
    all_to_all x1, starting transfers between devices, per_device(): mine = lax.all_to_all(messages, wide, 0, 0, tiled=True)  23.2 us
    all_to_all x1, waiting for transfers between devices, per_device(): mine = lax.all_to_all(messages, wide, 0, 0, tiled=True)  14.5 us
    ppermute x2, starting transfers between devices, swap_cores(): return lax.ppermute(block, 'core', [(0, 1), (1, 0)])  6.83 us
    pallas_call x1, Pallas kernels, grad_call(): pl.pallas_call(functools.partial(grad_kernel, core_axis='core', chunk=chu...  6.83 us
    unnamed x8, local copies, waits for them, and re-layouts  3.41 us
  transfers between devices with their start and end apart: 3, of which 3 were waited for; matrix products, arithmetic and copies ran while one was open for 0% of the time, Pallas kernels for 2%

profile of v5, /device:TPU:1, one launch (start us, length us, event | category | flops | bytes accessed | tf_op | source)
XLA Modules:
  0.0 91.5 jit_solution(230362145018273932)
XLA Ops:
  0.6 1.6 %shard_map.119 = bf16[2048,128]{1,0:T(8,128)(2,1)} custom-call(bf16[4,1024]{1,0:T(4,128)(2,1)} %keys_ref.1, bf16[4,1024]{1,0:T(4,128)(2,1)} %values_ref.1), custom_call_target="tpu_custom_call" | custom-call | tf_op jit(solution)/shard_map/pallas_call | solution.py:393
  2.2 23.2 %all-to-all-start = ((bf16[256,8,128]{2,1,0:T(8,128)(2,1)}), bf16[256,8,128]{2,1,0:T(8,128)(2,1)S(1)}, u32[]{:S(2)}, u32[]{:S(2)}) async-start(bf16[256,8,128]{2,1,0:T(8,128)(2,1)} %bitcast.12), calls=%async_computation | async-start | bytes 1048576 | tf_op jit(solution)/shard_map/all_to_all | solution.py:400
  26.7 0.0 copy-start
  26.7 0.9 %copy-done = bf16[128,1024]{1,0:T(8,128)(2,1)S(1)} copy-done((bf16[128,1024]{1,0:T(8,128)(2,1)S(1)}, bf16[128,1024]{1,0:T(8,128)(2,1)}, u32[]{:S(2)}) %copy-start) | copy-done | bytes 262168
  27.7 0.0 copy-start.1
  27.7 0.9 %copy-done.1 = bf16[128,1024]{1,0:T(8,128)(2,1)S(1)} copy-done((bf16[128,1024]{1,0:T(8,128)(2,1)S(1)}, bf16[128,1024]{1,0:T(8,128)(2,1)}, u32[]{:S(2)}) %copy-start.1) | copy-done | bytes 262168
  28.6 0.0 copy-start.2
  28.6 0.8 copy-done.2
  29.4 0.0 copy-start.3
  29.4 0.8 copy-done.3
  30.1 0.1 shard_map.120
  30.2 14.5 %all-to-all-done = bf16[256,8,128]{2,1,0:T(8,128)(2,1)S(1)} async-done(((bf16[256,8,128]{2,1,0:T(8,128)(2,1)}), bf16[256,8,128]{2,1,0:T(8,128)(2,1)S(1)}, u32[]{:S(2)}, u32[]{:S(2)}) %all-to-all-start) | async-done | bytes 524320 | tf_op jit(solution)/shard_map/all_to_all | solution.py:400
  44.8 4.6 %collective-permute-start = (bf16[2048,128]{1,0:T(8,128)(2,1)S(1)}, bf16[2048,128]{1,0:T(8,128)(2,1)S(1)}, u32[]{:S(2)}, u32[]{:S(2)}) collective-permute-start(bf16[2048,128]{1,0:T(8,128)(2,1)S(1)} %bitcast.9), channel_id=1, source_target_pairs={{0,1},{1,0},{2,3},{3,2},{4,5},{5,4},{6,7},{7,6},{8,9},{9,8},{10,11... | collective-permute-start | bytes 1572872 | tf_op jit(solution)/shard_map/ppermute | solution.py:386
  49.3 1.3 %shard_map.121 = (bf16[1152,128]{1,0:T(8,128)(2,1)}, bf16[1152,128]{1,0:T(8,128)(2,1)S(1)}, bf16[128,1152]{1,0:T(8,128)(2,1)S(1)}, f32[1152,1024]{1,0:T(8,128)S(1)}, f32[8,1024]{1,0:T(8,128)S(1)}) custom-call(s32[8,512]{1,0:T(8,128)S(1)} %get-tuple-element.37.seen_ref, bf16[1024,128]{1,0:T(8,128)(2,1)S(1)} %get-tuple-element.38.q_ref, ...), custom_call_target="tpu_custom_call" | custom-call | tf_op jit(solution)/shard_map/pallas_call | solution.py:308
  50.7 0.2 collective-permute-done.theirs_ref
  50.8 6.8 %shard_map.122 = (f32[128,1024]{1,0:T(8,128)S(1)}, f32[128,128]{1,0:T(8,128)S(1)}, f32[128,128]{1,0:T(8,128)S(1)}, bf16[2048,128]{1,0:T(8,128)(2,1)S(1)}, bf16[2048,128]{1,0:T(8,128)(2,1)S(1)}) custom-call(s32[8,512]{1,0:T(8,128)S(1)} %get-tuple-element.37.seen_ref, bf16[1024,128]{1,0:T(8,128)(2,1)S(1)} %get-tuple-element.38.q_ref, ...), custom_call_target="tpu_custom_call" | custom-call | tf_op jit(solution)/shard_map/pallas_call | solution.py:327
  57.7 2.3 %collective-permute-start.1 = (bf16[2048,128]{1,0:T(8,128)(2,1)S(1)}, bf16[2048,128]{1,0:T(8,128)(2,1)S(1)}, u32[]{:S(2)}, u32[]{:S(2)}) collective-permute-start(bf16[2048,128]{1,0:T(8,128)(2,1)S(1)} %get-tuple-element.51), channel_id=1, source_target_pairs={{0,1},{1,0},{2,3},{3,2},{4,5},{5,4},{6,7},{7,6},{8,9},{9,8},{10,11... | collective-permute-start | bytes 1572872 | tf_op jit(solution)/shard_map/ppermute | solution.py:386
  60.0 0.8 shard_map.123
  60.8 0.7 collective-permute-done.1
  61.5 0.1 fusion
  61.6 29.2 %all_to_all.23 = bf16[256,8,128]{2,1,0:T(8,128)(2,1)S(1)} all-to-all(bf16[256,8,128]{2,1,0:T(8,128)(2,1)S(1)} %fusion), channel_id=1, replica_groups=mesh['head'=8,'x'=4,'y'=8,'core'=2] {'head','x','y'}, dimensions={0} | all-to-all | bytes 1048576 | tf_op jit(solution)/shard_map/all_to_all | solution.py:410
  90.8 0.7 shard_map.124
Async XLA Ops:
  2.2 42.6 %all-to-all-start = ((bf16[256,8,128]{2,1,0:T(8,128)(2,1)}), bf16[256,8,128]{2,1,0:T(8,128)(2,1)S(1)}, u32[]{:S(2)}, u32[]{:S(2)}) async-start(bf16[256,8,128]{2,1,0:T(8,128)(2,1)} %bitcast.12), calls=%async_computation | async-start | bytes 1048576 | tf_op jit(solution)/shard_map/all_to_all | solution.py:400
  26.7 1.0 %copy-start = (bf16[128,1024]{1,0:T(8,128)(2,1)S(1)}, bf16[128,1024]{1,0:T(8,128)(2,1)}, u32[]{:S(2)}) copy-start(bf16[128,1024]{1,0:T(8,128)(2,1)} %q_ref.1) | copy-start | bytes 786436
  27.7 0.9 %copy-start.1 = (bf16[128,1024]{1,0:T(8,128)(2,1)S(1)}, bf16[128,1024]{1,0:T(8,128)(2,1)}, u32[]{:S(2)}) copy-start(bf16[128,1024]{1,0:T(8,128)(2,1)} %g_ref.1) | copy-start | bytes 786436
  28.6 0.8 copy-start.2
  29.4 0.8 copy-start.3
  44.8 6.1 %collective-permute-start = (bf16[2048,128]{1,0:T(8,128)(2,1)S(1)}, bf16[2048,128]{1,0:T(8,128)(2,1)S(1)}, u32[]{:S(2)}, u32[]{:S(2)}) collective-permute-start(bf16[2048,128]{1,0:T(8,128)(2,1)S(1)} %bitcast.9), channel_id=1, source_target_pairs={{0,1},{1,0},{2,3},{3,2},{4,5},{5,4},{6,7},{7,6},{8,9},{9,8},{10,11... | collective-permute-start | bytes 1572872 | tf_op jit(solution)/shard_map/ppermute | solution.py:386
  57.7 3.8 %collective-permute-start.1 = (bf16[2048,128]{1,0:T(8,128)(2,1)S(1)}, bf16[2048,128]{1,0:T(8,128)(2,1)S(1)}, u32[]{:S(2)}, u32[]{:S(2)}) collective-permute-start(bf16[2048,128]{1,0:T(8,128)(2,1)S(1)} %get-tuple-element.51), channel_id=1, source_target_pairs={{0,1},{1,0},{2,3},{3,2},{4,5},{5,4},{6,7},{7,6},{8,9},{9,8},{10,11... | collective-permute-start | bytes 1572872 | tf_op jit(solution)/shard_map/ppermute | solution.py:386

commit v6 on v5

--- a/solution.py
+++ b/solution.py
@@ -107,6 +107,7 @@
 def early_kernel(
     seen_ref,
     q_ref,
+    g_ref,
     own_k_ref,
     own_v_ref,
     mine_ref,
@@ -115,6 +116,7 @@
     kt_ref,
     s_ref,
     peak_ref,
+    p_ref,
     *,
     core_axis,
     chunk,
@@ -143,6 +145,7 @@
             s_ref[row : row + size, rows] = s
             peak = jnp.maximum(peak, fold(s, jnp.max))
         peak_ref[:, rows] = peak
+        p_ref[:, rows] = dot(v_ref[0 : p_ref.shape[0], :], g_ref[rows, :], NT)
 
 
 def grad_kernel(
@@ -153,6 +156,7 @@
     kt_ref,
     s_ref,
     peak_ref,
+    p_ref,
     theirs_ref,
     dqt_ref,
     dok_ref,
@@ -220,10 +224,14 @@
             else:
                 values = v_s[row - kept : row - kept + size, :]
                 s = self.w[row : row + size, :]
-            gp = dot(values, self.g, NT)
+            ready = row < p_ref.shape[0]
+            if ready:
+                gp = p_ref[row : row + size, self.rows]
+            else:
+                gp = dot(values, self.g, NT)
+                self.p[row : row + size, :] = gp
             w = jnp.exp2((s - self.peak) * scale)
             self.w[row : row + size, :] = w
-            self.p[row : row + size, :] = gp
             self.total = self.total + fold(w, jnp.sum)
             self.weighted = self.weighted + fold(w * gp, jnp.sum)
 
@@ -233,7 +241,11 @@
 
         def grad(self, row, size):
             probs = self.w[row : row + size, :] * self.inverse
-            grads = probs * (self.p[row : row + size, :] - self.delta)
+            if row < p_ref.shape[0]:
+                gp = p_ref[row : row + size, self.rows]
+            else:
+                gp = self.p[row : row + size, :]
+            grads = probs * (gp - self.delta)
             probs = probs.astype(BF16)
             grads = grads.astype(BF16)
             if row < kept:
@@ -303,7 +315,7 @@
     )(lengths.reshape(1, 1), seen.reshape(1, 1), queries, cotangent, own_keys, own_values)
 
 
-def early_call(seen, q, own_keys, own_values, mine, chunk=512, span=SPAN):
+def early_call(seen, q, g, own_keys, own_values, mine, chunk=256, span=SPAN):
     kept = own_keys.shape[0] + mine.shape[0] // 2
     return pl.pallas_call(
         functools.partial(early_kernel, core_axis="core", chunk=chunk, span=span),
@@ -313,14 +325,15 @@
             jax.ShapeDtypeStruct((128, kept), BF16),
             jax.ShapeDtypeStruct((kept, q.shape[0]), F32),
             jax.ShapeDtypeStruct((TILE, q.shape[0]), F32),
-        ),
-        in_specs=[VMEM] * 5,
-        out_specs=(VMEM,) * 5,
+            jax.ShapeDtypeStruct((own_keys.shape[0] + 512, q.shape[0]), F32),
+        ),
+        in_specs=[VMEM] * 6,
+        out_specs=(VMEM,) * 6,
         compiler_params=megabytes(8),
-    )(seen, q, own_keys, own_values, mine)
-
-
-def grad_call(seen, q, g, values, keys_t, scores, peak, theirs, tokens, chunk=512, span=SPAN):
+    )(seen, q, g, own_keys, own_values, mine)
+
+
+def grad_call(seen, q, g, values, keys_t, scores, peak, products, theirs, tokens, chunk=512, span=SPAN):
     stacked = q.shape[0]
     half = theirs.shape[0] // 2
     key_count = tokens + 2 * half
@@ -333,7 +346,7 @@
             jax.ShapeDtypeStruct(theirs.shape, BF16),
             jax.ShapeDtypeStruct(theirs.shape, BF16),
         ),
-        in_specs=[VMEM] * 8,
+        in_specs=[VMEM] * 9,
         out_specs=(VMEM,) * 5,
         scratch_shapes=[
             pltpu.VMEM((half, 128), BF16),
@@ -345,7 +358,7 @@
             pltpu.VMEM((key_count, 128), F32),
         ],
         compiler_params=megabytes(36),
-    )(seen, q, g, values, keys_t, scores, peak, theirs)
+    )(seen, q, g, values, keys_t, scores, peak, products, theirs)
 
 
 def finish_kernel(dqt_ref, dk_ref, dv_ref, dq_ref, dok_ref, dov_ref):
@@ -402,7 +415,7 @@
     mine, staged = lax.optimization_barrier((mine, staged))
     theirs = swap_cores(mine)
     q, g, seen, held_keys, held_values = staged
-    early = early_call(seen, q, held_keys, held_values, mine)
+    early = early_call(seen, q, g, held_keys, held_values, mine)
     dqt, dk, dv, dmine, dtheirs = grad_call(seen, q, g, *early[1:], theirs, own_keys.shape[0])
     dq, dok, dov = finish_call(dqt, dk, dv, queries.shape)
     arrived, dok = lax.optimization_barrier((swap_cores(dtheirs), dok))

time: 92 us -> 91.8 us (level)
  no operation moved by 1% of the time
where the time goes in v6:
time: 91.8 us; the launch traced here: 91.3 us
  starting transfers between devices  30.2 us (33%)
  blocking collectives  29 us (32%)
  waiting for transfers between devices  15.4 us (17%)
  Pallas kernels  11.2 us (12%)
  local copies, waits for them, and re-layouts  3.41 us (4%)
  between operations  1.98 us (2%)
    all_to_all x1, blocking collectives, per_device(): back = lax.all_to_all(summed, wide, 0, 0, tiled=True)  29 us
    all_to_all x1, starting transfers between devices, per_device(): mine = lax.all_to_all(messages, wide, 0, 0, tiled=True)  23.2 us
    all_to_all x1, waiting for transfers between devices, per_device(): mine = lax.all_to_all(messages, wide, 0, 0, tiled=True)  14.5 us
    ppermute x2, starting transfers between devices, swap_cores(): return lax.ppermute(block, 'core', [(0, 1), (1, 0)])  7.02 us
    pallas_call x1, Pallas kernels, grad_call(): pl.pallas_call(functools.partial(grad_kernel, core_axis='core', chunk=chu...  6.8 us
    unnamed x8, local copies, waits for them, and re-layouts  3.41 us
  transfers between devices with their start and end apart: 3, of which 3 were waited for; matrix products, arithmetic and copies ran while one was open for 0% of the time, Pallas kernels for 2%

profile of v6, /device:TPU:1, one launch (start us, length us, event | category | flops | bytes accessed | tf_op | source)
XLA Modules:
  0.0 91.3 jit_solution(2526427844240773378)
XLA Ops:
  0.6 1.6 %shard_map.119 = bf16[2048,128]{1,0:T(8,128)(2,1)} custom-call(bf16[4,1024]{1,0:T(4,128)(2,1)} %keys_ref.1, bf16[4,1024]{1,0:T(4,128)(2,1)} %values_ref.1), custom_call_target="tpu_custom_call" | custom-call | tf_op jit(solution)/shard_map/pallas_call | solution.py:406
  2.2 23.2 %all-to-all-start = ((bf16[256,8,128]{2,1,0:T(8,128)(2,1)}), bf16[256,8,128]{2,1,0:T(8,128)(2,1)S(1)}, u32[]{:S(2)}, u32[]{:S(2)}) async-start(bf16[256,8,128]{2,1,0:T(8,128)(2,1)} %bitcast.12), calls=%async_computation | async-start | bytes 1048576 | tf_op jit(solution)/shard_map/all_to_all | solution.py:413
  26.7 0.0 copy-start
  26.7 0.9 %copy-done = bf16[128,1024]{1,0:T(8,128)(2,1)S(1)} copy-done((bf16[128,1024]{1,0:T(8,128)(2,1)S(1)}, bf16[128,1024]{1,0:T(8,128)(2,1)}, u32[]{:S(2)}) %copy-start) | copy-done | bytes 262168
  27.7 0.0 copy-start.1
  27.7 0.9 %copy-done.1 = bf16[128,1024]{1,0:T(8,128)(2,1)S(1)} copy-done((bf16[128,1024]{1,0:T(8,128)(2,1)S(1)}, bf16[128,1024]{1,0:T(8,128)(2,1)}, u32[]{:S(2)}) %copy-start.1) | copy-done | bytes 262168
  28.6 0.0 copy-start.2
  28.6 0.8 copy-done.2
  29.4 0.0 copy-start.3
  29.4 0.8 copy-done.3
  30.1 0.1 shard_map.120
  30.2 14.5 %all-to-all-done = bf16[256,8,128]{2,1,0:T(8,128)(2,1)S(1)} async-done(((bf16[256,8,128]{2,1,0:T(8,128)(2,1)}), bf16[256,8,128]{2,1,0:T(8,128)(2,1)S(1)}, u32[]{:S(2)}, u32[]{:S(2)}) %all-to-all-start) | async-done | bytes 524320 | tf_op jit(solution)/shard_map/all_to_all | solution.py:413
  44.8 4.6 %collective-permute-start = (bf16[2048,128]{1,0:T(8,128)(2,1)S(1)}, bf16[2048,128]{1,0:T(8,128)(2,1)S(1)}, u32[]{:S(2)}, u32[]{:S(2)}) collective-permute-start(bf16[2048,128]{1,0:T(8,128)(2,1)S(1)} %bitcast.9), channel_id=1, source_target_pairs={{0,1},{1,0},{2,3},{3,2},{4,5},{5,4},{6,7},{7,6},{8,9},{9,8},{10,11... | collective-permute-start | bytes 1572872 | tf_op jit(solution)/shard_map/ppermute | solution.py:399
  49.3 1.2 %shard_map.121 = (bf16[1152,128]{1,0:T(8,128)(2,1)}, bf16[1152,128]{1,0:T(8,128)(2,1)S(1)}, bf16[128,1152]{1,0:T(8,128)(2,1)S(1)}, f32[1152,1024]{1,0:T(8,128)S(...) custom-call(s32[8,512]{1,0:T(8,128)S(1)} %get-tuple-element.38.seen_ref, ...), custom_call_target="tpu_custom_call" | custom-call | tf_op jit(solution)/shard_map/pallas_call | solution.py:320
  50.5 0.3 collective-permute-done.theirs_ref
  50.8 6.8 %shard_map.122 = (f32[128,1024]{1,0:T(8,128)S(1)}, f32[128,128]{1,0:T(8,128)S(1)}, f32[128,128]{1,0:T(8,128)S(1)}, bf16[2048,128]{1,0:T(8,128)(2,1)S(1)}, bf16[2048,128]{1,0:T(8,128)(2,1)S(1)}) custom-call(s32[8,512]{1,0:T(8,128)S(1)} %get-tuple-element.38.seen_ref, bf16[1024,128]{1,0:T(8,128)(2,1)S(1)} %get-tuple-element.39.q_ref, ...), custom_call_target="tpu_custom_call" | custom-call | tf_op jit(solution)/shard_map/pallas_call | solution.py:340
  57.7 2.5 %collective-permute-start.1 = (bf16[2048,128]{1,0:T(8,128)(2,1)S(1)}, bf16[2048,128]{1,0:T(8,128)(2,1)S(1)}, u32[]{:S(2)}, u32[]{:S(2)}) collective-permute-start(bf16[2048,128]{1,0:T(8,128)(2,1)S(1)} %get-tuple-element.53), channel_id=1, source_target_pairs={{0,1},{1,0},{2,3},{3,2},{4,5},{5,4},{6,7},{7,6},{8,9},{9,8},{10,11... | collective-permute-start | bytes 1572872 | tf_op jit(solution)/shard_map/ppermute | solution.py:399
  60.1 0.8 shard_map.123
  61.0 0.5 collective-permute-done.1
  61.5 0.1 fusion
  61.6 29.0 %all_to_all.23 = bf16[256,8,128]{2,1,0:T(8,128)(2,1)S(1)} all-to-all(bf16[256,8,128]{2,1,0:T(8,128)(2,1)S(1)} %fusion), channel_id=1, replica_groups=mesh['head'=8,'x'=4,'y'=8,'core'=2] {'head','x','y'}, dimensions={0} | all-to-all | bytes 1048576 | tf_op jit(solution)/shard_map/all_to_all | solution.py:423
  90.6 0.7 shard_map.124
Async XLA Ops:
  2.2 42.6 %all-to-all-start = ((bf16[256,8,128]{2,1,0:T(8,128)(2,1)}), bf16[256,8,128]{2,1,0:T(8,128)(2,1)S(1)}, u32[]{:S(2)}, u32[]{:S(2)}) async-start(bf16[256,8,128]{2,1,0:T(8,128)(2,1)} %bitcast.12), calls=%async_computation | async-start | bytes 1048576 | tf_op jit(solution)/shard_map/all_to_all | solution.py:413
  26.7 1.0 %copy-start = (bf16[128,1024]{1,0:T(8,128)(2,1)S(1)}, bf16[128,1024]{1,0:T(8,128)(2,1)}, u32[]{:S(2)}) copy-start(bf16[128,1024]{1,0:T(8,128)(2,1)} %q_ref.1) | copy-start | bytes 786436
  27.7 0.9 %copy-start.1 = (bf16[128,1024]{1,0:T(8,128)(2,1)S(1)}, bf16[128,1024]{1,0:T(8,128)(2,1)}, u32[]{:S(2)}) copy-start(bf16[128,1024]{1,0:T(8,128)(2,1)} %g_ref.1) | copy-start | bytes 786436
  28.6 0.8 copy-start.2
  29.4 0.8 copy-start.3
  44.8 6.1 %collective-permute-start = (bf16[2048,128]{1,0:T(8,128)(2,1)S(1)}, bf16[2048,128]{1,0:T(8,128)(2,1)S(1)}, u32[]{:S(2)}, u32[]{:S(2)}) collective-permute-start(bf16[2048,128]{1,0:T(8,128)(2,1)S(1)} %bitcast.9), channel_id=1, source_target_pairs={{0,1},{1,0},{2,3},{3,2},{4,5},{5,4},{6,7},{7,6},{8,9},{9,8},{10,11... | collective-permute-start | bytes 1572872 | tf_op jit(solution)/shard_map/ppermute | solution.py:399
  57.7 3.8 %collective-permute-start.1 = (bf16[2048,128]{1,0:T(8,128)(2,1)S(1)}, bf16[2048,128]{1,0:T(8,128)(2,1)S(1)}, u32[]{:S(2)}, u32[]{:S(2)}) collective-permute-start(bf16[2048,128]{1,0:T(8,128)(2,1)S(1)} %get-tuple-element.53), channel_id=1, source_target_pairs={{0,1},{1,0},{2,3},{3,2},{4,5},{5,4},{6,7},{7,6},{8,9},{9,8},{10,11... | collective-permute-start | bytes 1572872 | tf_op jit(solution)/shard_map/ppermute | solution.py:399
